TPU v7x, 512 devices: a whole 4x4x16 slice. The times are simulated.
512 devices in a mesh: row: 16 (over y, x), col: 32 (over z, core).
Axes of the slice: x: 4, y: 4, z: 16, core: 2. Of those that a mesh axis runs over, the one named last changes fastest.
Arguments:
- three_centre: bfloat16 [256, 1024, 1024], P('col', 'row'), may hold values from -6 to 6
- density: bfloat16 [1024, 1024], P('col'), may hold values from -0.00036621094 to 0.00036621094
- pair_mask: int32 [16, 16], replicated, may hold values 0 or 1
- density_mask: int32 [16, 16], replicated, may hold values 0 or 1
Outputs:
- exchange_matrix: float32 [1024, 1024], P('row', 'col')
All inputs are finite; a program needn't handle non-finite values.
Results may differ from a plain program's by a relative error of at most 0.0029.
Values may be sent and summed in bfloat16 or wider, within the bound.
No kernel may reach another device: no remote copies, remote signals or barrier semaphores. Data moves between devices by JAX's collectives and lax.ppermute only.
A program may use at most 64 MiB of HBM per device.

v0:
```python
import jax
import jax.numpy as jnp
from jax import lax
from jax.sharding import PartitionSpec as P


def body(three_centre, density, pair_mask, density_mask):
    aux_local, block_size, basis_size = three_centre.shape
    block_count = pair_mask.shape[0]
    row_index = lax.axis_index("row")
    col_index = lax.axis_index("col")
    block_ids = jnp.arange(block_count, dtype=jnp.int32)
    lam_column = lax.dynamic_slice_in_dim(pair_mask, row_index, 1, 1)[:, 0]
    mu_scale = jnp.repeat(lam_column.astype(jnp.float32), block_size).astype(jnp.bfloat16)
    stored = three_centre * mu_scale[None, None, :]
    density_rows = density.shape[0]
    row_blocks = (
        col_index * density_rows + jnp.arange(density_rows, dtype=jnp.int32)
    ) // block_size
    one_hot = (row_blocks[:, None] == block_ids[None, :]).astype(jnp.float32)
    row_masks = jnp.dot(one_hot, density_mask.astype(jnp.float32))
    density_scale = jnp.repeat(row_masks, block_size, axis=1).astype(jnp.bfloat16)
    masked_density = density * density_scale
    full_density = lax.all_gather(masked_density, "col", axis=0, tiled=True)
    pieces = lax.all_to_all(stored, "row", split_axis=2, concat_axis=1, tiled=True)
    half_built = jnp.einsum(
        "plm,ls->pms", pieces, full_density, preferred_element_type=jnp.float32
    ).astype(jnp.bfloat16)
    outer_view = jnp.swapaxes(pieces, 1, 2)
    product = jnp.einsum(
        "pms,pns->mn",
        half_built,
        lax.all_gather(outer_view, "row", axis=1, tiled=True),
        preferred_element_type=jnp.float32,
    )
    return lax.psum_scatter(product, "col", scatter_dimension=1, tiled=True)


def solution(mesh):
    return jax.shard_map(
        body,
        mesh=mesh,
        in_specs=(P("col", "row", None), P("col", None), P(), P()),
        out_specs=P("row", "col"),
        check_vma=False,
    )
```

profile of v0, /device:TPU:1, one launch (start us, length us, event | category | flops | bytes accessed | tf_op | source)
XLA Modules:
  0.0 340.4 jit_solution(9187709785478324579)
XLA Ops:
  6.5 0.0 all-gather.3.cloned.1.call-start
  6.5 0.9 convolution_convert_fusion
  7.4 0.1 copy.14
  7.5 0.2 broadcast_in_dim.10
  7.7 0.1 convert_element_type.38
  7.8 1.5 mul.17
  9.3 0.0 all-gather.3.cloned.1.call-update
  9.3 0.0 all-gather.5.cloned.1.call-start
  9.4 0.9 fusion.9
  10.3 0.1 broadcast_in_dim.4
  10.3 0.1 convert_element_type.35
  10.4 1.3 broadcast_multiply_fusion
  11.7 1.7 copy.12
  13.4 1.5 reshape.33
  14.9 21.8 %all_to_all.18 = bf16[16,2,16384]{2,1,0:T(2,128)(2,1)} all-to-all(bf16[16,2,16384]{2,1,0:T(2,128)(2,1)S(1)} %reshape.33), channel_id=1, replica_groups=mesh['row'=16,'col'=32] {'row'}, dimensions={0} | all-to-all | bytes 2097152 | tf_op jit(solution)/shard_map/all_to_all | solution.py:25
  36.7 3.8 %reshape.34 = bf16[1024,8,64]{2,1,0:T(8,128)(2,1)S(1)} reshape(bf16[16,2,16384]{2,1,0:T(2,128)(2,1)} %all_to_all.18) | data formatting | bytes 2097152
  40.5 2.7 copy.16
  43.2 4.1 %all_to_all.16 = bf16[8,1024,64]{1,2,0:T(8,128)(2,1)} reshape(bf16[8,16,64,64]{2,1,3,0:T(8,128)(2,1)} %bitcast.24) | data formatting | bytes 2097152 | tf_op jit(solution)/shard_map/all_to_all | solution.py:25
  47.3 0.0 all-gather.5.cloned.1.call-update
  47.3 0.0 reduce-scatter.2.cloned.1.call-start
  47.4 39.7 %all-gather.3.cloned.1.call-done = bf16[1024,1024]{1,0:T(8,128)(2,1)} async-done(((bf16[32,1024]{1,0:T(8,128)(2,1)}), bf16[1024,1024]{1,0:T(8,128)(2,1)}) %all-gather.3.cloned.1.call-update) | async-done | bytes 2097168 | tf_op jit(solution)/shard_map/all_gather | solution.py:24
  87.1 126.1 %all-gather.5.cloned.1.call-done = bf16[8,1024,1024]{2,1,0:T(8,128)(2,1)} async-done(((bf16[8,64,1024]{2,1,0:T(8,128)(2,1)}), bf16[8,1024,1024]{2,1,0:T(8,128)(2,1)}) %all-gather.5.cloned.1.call-update) | async-done | bytes 16777232 | tf_op jit(solution)/shard_map/all_gather | solution.py:33
  213.3 16.2 %convolution_bitcast_fusion = f32[64,1024]{0,1:T(8,128)} fusion(bf16[8,1024,1024]{2,1,0:T(8,128)(2,1)} %all-gather.5.cloned.1.call-done, bf16[8,1024,64]{1,2,0:T(8,128)(2,1)} %all_to_all.16, bf16[1024,1024]{1,0:T(8,128)(2,1)} %all-gather.3.cloned.1.call-done), kind=kOutput, calls=%fused_computation.4 | convolution fusion | flops 2148007936 | bytes 20185088 | tf_op jit(solution)/shard_map/pms,pns->mn/dot_general | solution.py:30
  229.4 0.0 reduce-scatter.2.cloned.1.call-update
  229.4 104.4 %reduce-scatter.2.cloned.1.call-done = f32[64,32]{0,1:T(8,128)} async-done(((f32[64,1024]{0,1:T(8,128)}), f32[64,32]{0,1:T(8,128)}) %reduce-scatter.2.cloned.1.call-update) | async-done | bytes 8208 | tf_op jit(solution)/shard_map/reduce_scatter | solution.py:36
  (1 shorter events, 0.0 us)
Async XLA Ops:
  6.5 80.6 %all-gather.3.cloned.1.call-start = ((), (), s32[]{:S(2)}) async-start(), calls=%async_computation.2 | async-start | bytes 2162688 | tf_op jit(solution)/shard_map/all_gather | solution.py:24
  9.3 203.9 %all-gather.5.cloned.1.call-start = ((), (), s32[]{:S(2)}) async-start(), calls=%async_computation.3 | async-start | bytes 17825792 | tf_op jit(solution)/shard_map/all_gather | solution.py:33
  47.3 286.5 %reduce-scatter.2.cloned.1.call-start = ((), (), s32[]{:S(2)}) async-start(), calls=%async_computation.4 | async-start | bytes 540672 | tf_op jit(solution)/shard_map/reduce_scatter | solution.py:36
Sparse Core Ops, SparseCore 0:
  9.5 77.5 all-gather.2
  90.1 123.0 all-gather.4
  229.6 104.2 reduce-scatter.1
where the time goes:
time: 343 us; the launch traced here: 340 us
  waiting for transfers between devices  270 us (79%)
  blocking collectives  21.8 us (6%)
  matrix products  17.1 us (5%)
  local copies, waits for them, and re-layouts  14.3 us (4%)
  between operations  13.2 us (4%)
  other arithmetic  3.67 us (1%)
    all_gather x1, waiting for transfers between devices, body(): lax.all_gather(outer_view, 'row', axis=1, tiled=True)  126 us
    reduce_scatter x1, waiting for transfers between devices, body(): return lax.psum_scatter(product, 'col', scatter_dimension=1, tiled=True)  104 us
    all_gather x1, waiting for transfers between devices, body(): full_density = lax.all_gather(masked_density, 'col', axis=0, tiled=True)  39.7 us
    all_to_all x1, blocking collectives, body(): lax.all_to_all(stored, 'row', split_axis=2, concat_axis=1, tiled=True)  21.8 us
    dot_general x1, matrix products, body(): jnp.einsum('pms,pns->mn', half_built, lax.all_gather(outer_view, 'row', a...  16.2 us
  transfers between devices with their start and end apart: 3, of which 3 were waited for; matrix products, arithmetic and copies ran while one was open for 4% of the time, Pallas kernels for 0%

commit v1 on v0

v1 whole, which is shorter than its diff:
```python
import functools

import jax
import jax.numpy as jnp
from jax import lax
from jax.experimental import pallas as pl
from jax.experimental.pallas import tpu as pltpu
from jax.sharding import Mesh
from jax.sharding import PartitionSpec as P

VMEM = pltpu.VMEM
SMEM = pltpu.SMEM
AXES = ("y", "x", "z", "core")
ROW = ("y", "x")
COL = ("z", "core")
BLK = 64
HALF = 32
LANES = 128


def vmem():
    return pl.BlockSpec(memory_space=VMEM)


def smem():
    return pl.BlockSpec(memory_space=SMEM)


def prepare(tc_ref, den_ref, pair_ref, dmask_ref, keep_ref, send_ref, den_out_ref):
    row = lax.axis_index("y") * 4 + lax.axis_index("x")
    core = lax.axis_index("core")
    aux, height, basis = tc_ref.shape
    wide = 2 * LANES
    src = lax.broadcasted_iota(jnp.int32, (wide, wide), 0)
    dst = lax.broadcasted_iota(jnp.int32, (wide, wide), 1)
    half = jnp.where(dst < LANES, core, 1 - core)
    lane = dst % LANES
    block = lane // HALF
    hit = src == block * BLK + half * HALF + lane % HALF
    rows = tc_ref[...].reshape(aux * height, basis)
    for tile in range(basis // wide):
        s = [pair_ref[4 * tile + b, row].astype(jnp.float32) for b in range(4)]
        scale = jnp.where(block == 0, s[0], jnp.where(block == 1, s[1], jnp.where(block == 2, s[2], s[3])))
        pick = jnp.where(hit, scale, 0.0).astype(jnp.bfloat16)
        out = jnp.dot(rows[:, tile * wide : (tile + 1) * wide], pick, preferred_element_type=jnp.float32)
        out = out.astype(jnp.bfloat16).reshape(aux, height, wide)
        keep_ref[:, :, tile * LANES : (tile + 1) * LANES] = out[:, :, :LANES]
        send_ref[:, :, tile * LANES : (tile + 1) * LANES] = out[:, :, LANES:]
    mask_row = lax.axis_index("z")
    low = lax.broadcasted_iota(jnp.int32, (den_ref.shape[0], LANES), 1) < BLK
    for tile in range(basis // LANES):
        cols = slice(tile * LANES, (tile + 1) * LANES)
        a = dmask_ref[mask_row, 2 * tile].astype(jnp.float32)
        b = dmask_ref[mask_row, 2 * tile + 1].astype(jnp.float32)
        scaled = den_ref[:, cols].astype(jnp.float32) * jnp.where(low, a, b)
        den_out_ref[:, cols] = scaled.astype(jnp.bfloat16)


def contract(own_ref, other_ref, den_ref, out_ref):
    core = lax.axis_index("core")
    parts, height, width = own_ref.shape
    own = own_ref[...].reshape(parts * height, width)
    built = lax.dot_general(
        own, den_ref[...], (((0,), (0,)), ((), ())), preferred_element_type=jnp.float32
    ).astype(jnp.bfloat16)
    other = other_ref[...].reshape(parts * height, width)
    shape = (out_ref.shape[0], out_ref.shape[1], width)
    mine = jnp.dot(built, own, preferred_element_type=jnp.float32).astype(jnp.bfloat16)
    out_ref[:, :, pl.ds(pl.multiple_of(core * width, LANES), width)] = mine.reshape(shape)
    theirs = jnp.dot(built, other, preferred_element_type=jnp.float32).astype(jnp.bfloat16)
    out_ref[:, :, pl.ds(pl.multiple_of((1 - core) * width, LANES), width)] = theirs.reshape(shape)


def gather_groups(groups, start):
    return jnp.concatenate([g[:, start : start + HALF] for g in groups], axis=1)


def sum_aux(in_ref, out_ref):
    basis = in_ref.shape[2]
    for tile in range(basis // LANES):
        cols = slice(tile * LANES, (tile + 1) * LANES)
        total = in_ref[0, :, cols].astype(jnp.float32)
        for k in range(1, in_ref.shape[0]):
            total = total + in_ref[k, :, cols].astype(jnp.float32)
        groups = [total[8 * g : 8 * g + 8] for g in range(4)]
        for q in range(4):
            dest = ((tile % 4) * 4 + q) * 2 + tile // 4
            out_ref[dest] = gather_groups(groups, q * HALF)


def sum_planes(in_ref, out_ref):
    for core in range(2):
        total = in_ref[core]
        for z in range(1, in_ref.shape[0] // 2):
            total = total + in_ref[2 * z + core]
        for g in range(4):
            out_ref[core * HALF + 8 * g : core * HALF + 8 * g + 8, :] = total[:, g * HALF : (g + 1) * HALF]


def body(three_centre, density, pair_mask, density_mask):
    aux, height, basis = three_centre.shape
    width = basis // 2
    bf16, f32 = jnp.bfloat16, jnp.float32
    core = lax.axis_index("core")
    swap = [(0, 1), (1, 0)]
    half = jax.ShapeDtypeStruct((aux, height, width), bf16)
    keep, send, masked_density = pl.pallas_call(
        prepare,
        out_shape=(half, half, jax.ShapeDtypeStruct(density.shape, bf16)),
        in_specs=[vmem(), vmem(), smem(), smem()],
        out_specs=(vmem(), vmem(), vmem()),
        compiler_params=pltpu.CompilerParams(vmem_limit_bytes=32 << 20),
        name="prepare",
    )(three_centre, density, pair_mask, density_mask)
    full_density = lax.all_gather(masked_density, COL, axis=0, tiled=True)
    got = lax.ppermute(send, "core", swap)
    slabs = jnp.where(core == 0, jnp.concatenate([keep, got]), jnp.concatenate([got, keep]))
    own = lax.all_to_all(slabs, ROW, 0, 0, tiled=True)
    other = lax.ppermute(own, "core", swap)
    partial = pl.pallas_call(
        contract,
        out_shape=jax.ShapeDtypeStruct((2 * aux, HALF, basis), bf16),
        in_specs=[vmem(), vmem(), vmem()],
        out_specs=vmem(),
        compiler_params=pltpu.CompilerParams(vmem_limit_bytes=48 << 20),
        name="contract",
    )(own, other, full_density)
    pieces = lax.all_to_all(partial, ROW, 0, 0, tiled=True)
    packed = pl.pallas_call(
        sum_aux,
        out_shape=jax.ShapeDtypeStruct((32, 8, LANES), f32),
        in_specs=[vmem()],
        out_specs=vmem(),
        compiler_params=pltpu.CompilerParams(vmem_limit_bytes=16 << 20),
        name="sum_aux",
    )(pieces)
    arrived = lax.all_to_all(packed, COL, 0, 0, tiled=True)
    return pl.pallas_call(
        sum_planes,
        out_shape=jax.ShapeDtypeStruct((BLK, HALF), f32),
        in_specs=[vmem()],
        out_specs=vmem(),
        compiler_params=pltpu.CompilerParams(vmem_limit_bytes=16 << 20),
        name="sum_planes",
    )(arrived)


def solution(mesh):
    fine = Mesh(mesh.devices.reshape(4, 4, 16, 2), AXES)
    return jax.shard_map(
        body,
        mesh=fine,
        in_specs=(P(COL, ROW, None), P(COL, None), P(), P()),
        out_specs=P(ROW, COL),
        check_vma=False,
    )
```

time: 343 us -> 150 us (0.44)
  waiting for transfers between devices: 270 us -> 46.1 us
  blocking collectives: 21.8 us -> 67.4 us
  matrix products: 17.1 us -> 0 us
  starting transfers between devices: 0.09 us -> 12.2 us
  local copies, waits for them, and re-layouts: 14.3 us -> 5.73 us
  Pallas kernels: 0 us -> 4.16 us
  other arithmetic: 3.67 us -> 0.16 us
    all_gather x2 -> x1, waiting for transfers between devices: 166 us -> 42.3 us  [body(): full_density = lax.all_gather(masked_density, COL, axis=0, tiled=True)]
    reduce_scatter x1 -> x0, waiting for transfers between devices: 104 us -> none  [body(): return lax.psum_scatter(product, 'col', scatter_dimension=1, tiled=True)]
    all_to_all x1 -> x3, blocking collectives: 21.8 us -> 67.4 us  [the longest x1 25.3 us: body(): arrived = lax.all_to_all(packed, COL, 0, 0, tiled=True)]
    dot_general x2 -> x0, matrix products: 17.1 us -> none  [the longest x1 16.2 us: body(): jnp.einsum('pms,pns->mn', half_built, lax.all_gather(outer_view, 'row', a...]
    ppermute x0 -> x2, starting transfers between devices: none -> 12.2 us  [the longest x1 8.79 us: body(): got = lax.ppermute(send, 'core', swap)]
    all_to_all x2 -> x0, local copies, waits for them, and re-layouts: 6.8 us -> none  [body(): lax.all_to_all(stored, 'row', split_axis=2, concat_axis=1, tiled=True)]
    pallas_call x0 -> x4, Pallas kernels: none -> 4.16 us  [the longest x1 2.35 us: body(): pl.pallas_call(contract, out_shape=jax.ShapeDtypeStruct((2 * aux, HALF, b...]
    ppermute x0 -> x2, waiting for transfers between devices: none -> 3.77 us  [the longest x1 2.26 us: body(): other = lax.ppermute(own, 'core', swap)]
  transfers between devices with their start and end apart: 3 -> 3, of which waited for: 3 -> 3; matrix products, arithmetic and copies ran while one was open for 4% -> 0% of each run, Pallas kernels for 0% -> 0%
where the time goes in v1:
time: 150 us; the launch traced here: 149 us
  blocking collectives  67.4 us (45%)
  waiting for transfers between devices  46.1 us (31%)
  between operations  13.4 us (9%)
  starting transfers between devices  12.2 us (8%)
  local copies, waits for them, and re-layouts  5.73 us (4%)
  Pallas kernels  4.16 us (3%)
    all_gather x1, waiting for transfers between devices, body(): full_density = lax.all_gather(masked_density, COL, axis=0, tiled=True)  42.3 us
    all_to_all x1, blocking collectives, body(): arrived = lax.all_to_all(packed, COL, 0, 0, tiled=True)  25.3 us
    all_to_all x1, blocking collectives, body(): pieces = lax.all_to_all(partial, ROW, 0, 0, tiled=True)  22.8 us
    all_to_all x1, blocking collectives, body(): own = lax.all_to_all(slabs, ROW, 0, 0, tiled=True)  19.3 us
    ppermute x1, starting transfers between devices, body(): got = lax.ppermute(send, 'core', swap)  8.79 us
    unnamed x10, local copies, waits for them, and re-layouts  5.05 us
    ppermute x1, starting transfers between devices, body(): other = lax.ppermute(own, 'core', swap)  3.39 us
  transfers between devices with their start and end apart: 3, of which 3 were waited for; matrix products, arithmetic and copies ran while one was open for 0% of the time, Pallas kernels for 0%

profile of v1, /device:TPU:1, one launch (start us, length us, event | category | flops | bytes accessed | tf_op | source)
XLA Modules:
  0.0 149.1 jit_solution(6631151868078901066)
XLA Ops:
  6.5 0.0 all-gather.2.cloned.1.call-start
  6.5 0.0 copy-start.1
  6.5 1.2 copy-done.1
  7.8 0.0 copy-start.2
  7.8 0.8 copy-done.2
  8.6 0.0 copy-start.3
  8.6 0.7 copy-done.3
  9.3 0.0 copy-start.4
  9.3 0.7 copy-done.4
  10.0 1.5 prepare.1
  11.5 0.0 all-gather.2.cloned.1.call-update
  11.5 8.8 %collective-permute-start = (bf16[8,64,512]{2,1,0:T(8,128)(2,1)S(1)}, bf16[8,64,512]{2,1,0:T(8,128)(2,1)S(1)}, u32[]{:S(2)}, u32[]{:S(2)}) collective-permute-start(bf16[8,64,512]{2,1,0:T(8,128)(2,1)S(1)} %get-tuple-element.9), channel_id=1, source_target_pairs={{0,1},{1,0},{2,3},{3,2},{4,5},{5,4},{6,7},{7,6},{8,9},{9,8},{10,11... | collective-permute-start | bytes 1572872 | tf_op jit(solution)/shard_map/ppermute | solution.py:116
  20.3 1.5 %collective-permute-done = bf16[8,64,512]{2,1,0:T(8,128)(2,1)S(1)} collective-permute-done((bf16[8,64,512]{2,1,0:T(8,128)(2,1)S(1)}, bf16[8,64,512]{2,1,0:T(8,128)(2,1)S(1)}, u32[]{:S(2)}, u32[]{:S(2)}) %collective-permute-start) | collective-permute-done | bytes 524320 | tf_op jit(solution)/shard_map/ppermute | solution.py:116
  21.8 0.2 maximum_select_fusion
  22.0 19.3 %all_to_all.15.own_ref = bf16[16,64,512]{2,1,0:T(8,128)(2,1)S(1)} all-to-all(bf16[16,64,512]{2,1,0:T(8,128)(2,1)S(1)} %maximum_select_fusion), channel_id=1, replica_groups=mesh['y'=4,'x'=4,'z'=16,'core'=2] {'y','x'}, dimensions={0} | all-to-all | bytes 2097152 | tf_op jit(solution)/shard_map/all_to_all | solution.py:118
  41.3 3.4 %collective-permute-start.1 = (bf16[16,64,512]{2,1,0:T(8,128)(2,1)S(1)}, bf16[16,64,512]{2,1,0:T(8,128)(2,1)S(1)}, u32[]{:S(2)}, u32[]{:S(2)}) collective-permute-start(bf16[16,64,512]{2,1,0:T(8,128)(2,1)S(1)} %all_to_all.15.own_ref), channel_id=1, source_target_pairs={{0,1},{1,0},{2,3},{3,2},{4,5},{5,4},{6,7},{7,6},{8,9},{9,8},{10,11... | collective-permute-start | bytes 3145736 | tf_op jit(solution)/shard_map/ppermute | solution.py:119
  44.7 2.3 %collective-permute-done.1.other_ref = bf16[16,64,512]{2,1,0:T(8,128)(2,1)S(1)} collective-permute-done((bf16[16,64,512]{2,1,0:T(8,128)(2,1)S(1)}, bf16[16,64,512]{2,1,0:T(8,128)(2,1)S(1)}, u32[]{:S(2)}, u32[]{:S(2)}) %collective-permute-start.1) | collective-permute-done | bytes 1048608 | tf_op jit(solution)/shard_map/ppermute | solution.py:119
  46.9 42.3 %all-gather.2.cloned.1.call-done.den_ref = bf16[1024,1024]{1,0:T(8,128)(2,1)} async-done(((bf16[32,1024]{1,0:T(8,128)(2,1)}), bf16[1024,1024]{1,0:T(8,128)(2,1)}) %all-gather.2.cloned.1.call-update) | async-done | bytes 2097168 | tf_op jit(solution)/shard_map/all_gather | solution.py:115
  89.2 0.0 copy-start
  89.2 1.6 %copy-done = bf16[1024,1024]{1,0:T(8,128)(2,1)S(1)} copy-done((bf16[1024,1024]{1,0:T(8,128)(2,1)S(1)}, bf16[1024,1024]{1,0:T(8,128)(2,1)}, u32[]{:S(2)}) %copy-start) | copy-done | bytes 2097176
  90.8 2.4 %contract.1 = bf16[16,32,1024]{2,1,0:T(8,128)(2,1)S(1)} custom-call(bf16[16,64,512]{2,1,0:T(8,128)(2,1)S(1)} %all_to_all.15.own_ref, bf16[16,64,512]{2,1,0:T(8,128)(2,1)S(1)} %collective-permute-done.1.other_ref, bf16[1024,1024]{1,0:T(8,128)(2,1)S(1)} %copy-done), custom_call_target="tpu_custom_call" | custom-call | tf_op jit(solution)/shard_map/contract/pallas_call | solution.py:120
  93.2 22.8 %all_to_all.16.in_ref = bf16[16,32,1024]{2,1,0:T(8,128)(2,1)S(1)} all-to-all(bf16[16,32,1024]{2,1,0:T(8,128)(2,1)S(1)} %contract.1), channel_id=1, replica_groups=mesh['y'=4,'x'=4,'z'=16,'core'=2] {'y','x'}, dimensions={0} | all-to-all | bytes 2097152 | tf_op jit(solution)/shard_map/all_to_all | solution.py:128
  116.0 0.2 sum_aux.1
  116.2 25.3 %all_to_all.17.in_ref = f32[32,8,128]{2,1,0:T(8,128)S(1)} all-to-all(f32[32,8,128]{2,1,0:T(8,128)S(1)} %sum_aux.1), channel_id=1, replica_groups=mesh['y'=4,'x'=4,'z'=16,'core'=2] {'z','core'}, dimensions={0} | all-to-all | bytes 262144 | tf_op jit(solution)/shard_map/all_to_all | solution.py:137
  141.5 0.1 sum_planes.1
  141.6 0.7 copy.5
Async XLA Ops:
  6.5 82.7 %all-gather.2.cloned.1.call-start = ((), (), s32[]{:S(2)}) async-start(), calls=%async_computation.3 | async-start | bytes 2162688 | tf_op jit(solution)/shard_map/all_gather | solution.py:115
  6.5 1.2 copy-start.1
  7.8 0.8 copy-start.2
  8.6 0.7 copy-start.3
  9.3 0.7 copy-start.4
  11.5 10.3 %collective-permute-start = (bf16[8,64,512]{2,1,0:T(8,128)(2,1)S(1)}, bf16[8,64,512]{2,1,0:T(8,128)(2,1)S(1)}, u32[]{:S(2)}, u32[]{:S(2)}) collective-permute-start(bf16[8,64,512]{2,1,0:T(8,128)(2,1)S(1)} %get-tuple-element.9), channel_id=1, source_target_pairs={{0,1},{1,0},{2,3},{3,2},{4,5},{5,4},{6,7},{7,6},{8,9},{9,8},{10,11... | collective-permute-start | bytes 1572872 | tf_op jit(solution)/shard_map/ppermute | solution.py:116
  41.3 5.7 %collective-permute-start.1 = (bf16[16,64,512]{2,1,0:T(8,128)(2,1)S(1)}, bf16[16,64,512]{2,1,0:T(8,128)(2,1)S(1)}, u32[]{:S(2)}, u32[]{:S(2)}) collective-permute-start(bf16[16,64,512]{2,1,0:T(8,128)(2,1)S(1)} %all_to_all.15.own_ref), channel_id=1, source_target_pairs={{0,1},{1,0},{2,3},{3,2},{4,5},{5,4},{6,7},{7,6},{8,9},{9,8},{10,11... | collective-permute-start | bytes 3145736 | tf_op jit(solution)/shard_map/ppermute | solution.py:119
  89.2 1.6 %copy-start = (bf16[1024,1024]{1,0:T(8,128)(2,1)S(1)}, bf16[1024,1024]{1,0:T(8,128)(2,1)}, u32[]{:S(2)}) copy-start(bf16[1024,1024]{1,0:T(8,128)(2,1)} %all-gather.2.cloned.1.call-done.den_ref) | copy-start | bytes 6291460
Sparse Core Ops, SparseCore 0:
  11.6 77.5 all-gather.1

commit v2 on v1

--- a/solution.py
+++ b/solution.py
@@ -1,5 +1,3 @@
-import functools
-
 import jax
 import jax.numpy as jnp
 from jax import lax
@@ -16,6 +14,7 @@
 BLK = 64
 HALF = 32
 LANES = 128
+PACK = 16
 
 
 def vmem():
@@ -26,7 +25,29 @@
     return pl.BlockSpec(memory_space=SMEM)
 
 
-def prepare(tc_ref, den_ref, pair_ref, dmask_ref, keep_ref, send_ref, den_out_ref):
+def first_density(den_hbm, dmask_hbm, piece_ref, den, dmask, sems):
+    row = lax.axis_index("y") * 4 + lax.axis_index("x")
+    tiles = den_hbm.shape[1] // LANES
+    tile = row % tiles
+    part = row // tiles
+    source = den_hbm.at[
+        pl.ds(pl.multiple_of(part * PACK, PACK), PACK), pl.ds(pl.multiple_of(tile * LANES, LANES), LANES)
+    ]
+    fetch_den = pltpu.make_async_copy(source, den, sems.at[0])
+    fetch_mask = pltpu.make_async_copy(dmask_hbm, dmask, sems.at[1])
+    fetch_den.start()
+    fetch_mask.start()
+    fetch_mask.wait()
+    fetch_den.wait()
+    low = lax.broadcasted_iota(jnp.int32, (PACK, LANES), 1) < BLK
+    mask_row = lax.axis_index("z")
+    a = dmask[mask_row, 2 * tile].astype(jnp.float32)
+    b = dmask[mask_row, 2 * tile + 1].astype(jnp.float32)
+    scaled = (den[...].astype(jnp.float32) * jnp.where(low, a, b)).astype(jnp.bfloat16)
+    piece_ref[...] = jnp.broadcast_to(scaled[None], piece_ref.shape)
+
+
+def prepare(tc_ref, pair_ref, keep_ref, send_ref):
     row = lax.axis_index("y") * 4 + lax.axis_index("x")
     core = lax.axis_index("core")
     aux, height, basis = tc_ref.shape
@@ -46,24 +67,40 @@
         out = out.astype(jnp.bfloat16).reshape(aux, height, wide)
         keep_ref[:, :, tile * LANES : (tile + 1) * LANES] = out[:, :, :LANES]
         send_ref[:, :, tile * LANES : (tile + 1) * LANES] = out[:, :, LANES:]
-    mask_row = lax.axis_index("z")
-    low = lax.broadcasted_iota(jnp.int32, (den_ref.shape[0], LANES), 1) < BLK
-    for tile in range(basis // LANES):
-        cols = slice(tile * LANES, (tile + 1) * LANES)
-        a = dmask_ref[mask_row, 2 * tile].astype(jnp.float32)
-        b = dmask_ref[mask_row, 2 * tile + 1].astype(jnp.float32)
-        scaled = den_ref[:, cols].astype(jnp.float32) * jnp.where(low, a, b)
-        den_out_ref[:, cols] = scaled.astype(jnp.bfloat16)
-
-
-def contract(own_ref, other_ref, den_ref, out_ref):
+
+
+def pack(keep_ref, got_ref, den_ref, out_ref):
     core = lax.axis_index("core")
-    parts, height, width = own_ref.shape
-    own = own_ref[...].reshape(parts * height, width)
+    aux, height, width = keep_ref.shape
+    out_ref[pl.ds(core * aux, aux), :height, :] = keep_ref[...]
+    out_ref[pl.ds((1 - core) * aux, aux), :height, :] = got_ref[...]
+    groups = width // LANES
+    each = den_ref.shape[0] // groups
+    for g in range(groups):
+        part = den_ref[each * g : each * (g + 1)].reshape(each * PACK, LANES)
+        spread = jnp.broadcast_to(part[None], (2 * aux, each * PACK, LANES))
+        out_ref[:, height:, g * LANES : (g + 1) * LANES] = spread
+
+
+def contract(own_ref, other_ref, out_ref, den):
+    core = lax.axis_index("core")
+    parts, both, width = own_ref.shape
+    height = both // 2
+    tiles = den.shape[-1] // LANES
+    groups = width // LANES
+    each = den.shape[0] // groups
+    for ref, side in ((own_ref, core), (other_ref, 1 - core)):
+        for k in range(2 * tiles):
+            cols = slice(k % tiles * LANES, (k % tiles + 1) * LANES)
+            for g in range(groups):
+                part = ref[k, height:, g * LANES : (g + 1) * LANES].reshape(each, PACK, LANES)
+                den[each * g : each * (g + 1), side, k // tiles, :, cols] = part
+    own = own_ref[:, :height, :].reshape(parts * height, width)
+    density = den[...].reshape(parts * height, den.shape[-1])
     built = lax.dot_general(
-        own, den_ref[...], (((0,), (0,)), ((), ())), preferred_element_type=jnp.float32
+        own, density, (((0,), (0,)), ((), ())), preferred_element_type=jnp.float32
     ).astype(jnp.bfloat16)
-    other = other_ref[...].reshape(parts * height, width)
+    other = other_ref[:, :height, :].reshape(parts * height, width)
     shape = (out_ref.shape[0], out_ref.shape[1], width)
     mine = jnp.dot(built, own, preferred_element_type=jnp.float32).astype(jnp.bfloat16)
     out_ref[:, :, pl.ds(pl.multiple_of(core * width, LANES), width)] = mine.reshape(shape)
@@ -89,42 +126,67 @@
 
 
 def sum_planes(in_ref, out_ref):
+    totals = []
     for core in range(2):
         total = in_ref[core]
         for z in range(1, in_ref.shape[0] // 2):
             total = total + in_ref[2 * z + core]
-        for g in range(4):
-            out_ref[core * HALF + 8 * g : core * HALF + 8 * g + 8, :] = total[:, g * HALF : (g + 1) * HALF]
+        totals += [total[:, g * HALF : (g + 1) * HALF] for g in range(4)]
+    out_ref[...] = jnp.concatenate(totals, axis=0).T
 
 
 def body(three_centre, density, pair_mask, density_mask):
     aux, height, basis = three_centre.shape
     width = basis // 2
     bf16, f32 = jnp.bfloat16, jnp.float32
-    core = lax.axis_index("core")
     swap = [(0, 1), (1, 0)]
+    planes = 16
+    piece = pl.pallas_call(
+        first_density,
+        out_shape=jax.ShapeDtypeStruct((planes, PACK, LANES), bf16),
+        in_specs=[pl.BlockSpec(memory_space=pltpu.HBM)] * 2,
+        out_specs=vmem(),
+        scratch_shapes=[
+            VMEM((PACK, LANES), bf16),
+            SMEM(density_mask.shape, jnp.int32),
+            pltpu.SemaphoreType.DMA((2,)),
+        ],
+        compiler_params=pltpu.CompilerParams(vmem_limit_bytes=60 << 20),
+        name="first_density",
+    )(density, density_mask)
+    piece, three_centre = lax.optimization_barrier((piece, three_centre))
+    along_z = lax.all_to_all(piece, "z", 0, 0, tiled=True)
     half = jax.ShapeDtypeStruct((aux, height, width), bf16)
-    keep, send, masked_density = pl.pallas_call(
+    keep, send = pl.pallas_call(
         prepare,
-        out_shape=(half, half, jax.ShapeDtypeStruct(density.shape, bf16)),
-        in_specs=[vmem(), vmem(), smem(), smem()],
-        out_specs=(vmem(), vmem(), vmem()),
+        out_shape=(half, half),
+        in_specs=[vmem(), smem()],
+        out_specs=(vmem(), vmem()),
         compiler_params=pltpu.CompilerParams(vmem_limit_bytes=32 << 20),
+        cost_estimate=pl.CostEstimate(flops=4 << 30, bytes_accessed=8 << 20, transcendentals=0),
         name="prepare",
-    )(three_centre, density, pair_mask, density_mask)
-    full_density = lax.all_gather(masked_density, COL, axis=0, tiled=True)
+    )(three_centre, pair_mask)
+    along_z, send = lax.optimization_barrier((along_z, send))
     got = lax.ppermute(send, "core", swap)
-    slabs = jnp.where(core == 0, jnp.concatenate([keep, got]), jnp.concatenate([got, keep]))
+    slabs = pl.pallas_call(
+        pack,
+        out_shape=jax.ShapeDtypeStruct((2 * aux, 2 * height, width), bf16),
+        in_specs=[vmem()] * 3,
+        out_specs=vmem(),
+        compiler_params=pltpu.CompilerParams(vmem_limit_bytes=32 << 20),
+        name="pack",
+    )(keep, got, along_z)
     own = lax.all_to_all(slabs, ROW, 0, 0, tiled=True)
     other = lax.ppermute(own, "core", swap)
     partial = pl.pallas_call(
         contract,
         out_shape=jax.ShapeDtypeStruct((2 * aux, HALF, basis), bf16),
-        in_specs=[vmem(), vmem(), vmem()],
-        out_specs=vmem(),
-        compiler_params=pltpu.CompilerParams(vmem_limit_bytes=48 << 20),
+        in_specs=[vmem()] * 2,
+        out_specs=vmem(),
+        scratch_shapes=[VMEM((planes, 2, 2, PACK, basis), bf16)],
+        compiler_params=pltpu.CompilerParams(vmem_limit_bytes=40 << 20),
         name="contract",
-    )(own, other, full_density)
+    )(own, other)
     pieces = lax.all_to_all(partial, ROW, 0, 0, tiled=True)
     packed = pl.pallas_call(
         sum_aux,
@@ -137,12 +199,12 @@
     arrived = lax.all_to_all(packed, COL, 0, 0, tiled=True)
     return pl.pallas_call(
         sum_planes,
-        out_shape=jax.ShapeDtypeStruct((BLK, HALF), f32),
+        out_shape=jax.ShapeDtypeStruct((HALF, BLK), f32),
         in_specs=[vmem()],
         out_specs=vmem(),
         compiler_params=pltpu.CompilerParams(vmem_limit_bytes=16 << 20),
         name="sum_planes",
-    )(arrived)
+    )(arrived).T
 
 
 def solution(mesh):

time: 150 us -> 120 us (0.80)
  waiting for transfers between devices: 46.1 us -> 13.8 us
  between operations: 13.4 us -> 0.07 us
  starting transfers between devices: 12.2 us -> 23.4 us
  blocking collectives: 67.4 us -> 73.6 us
  local copies, waits for them, and re-layouts: 5.73 us -> 1.92 us
  Pallas kernels: 4.16 us -> 6.54 us
    all_gather x1 -> x0, waiting for transfers between devices: 42.3 us -> none  [body(): full_density = lax.all_gather(masked_density, COL, axis=0, tiled=True)]
    all_to_all x0 -> x1, starting transfers between devices: none -> 15.8 us  [body(): along_z = lax.all_to_all(piece, 'z', 0, 0, tiled=True)]
    all_to_all x1, blocking collectives: 19.3 us -> 34.1 us  [body(): own = lax.all_to_all(slabs, ROW, 0, 0, tiled=True)]
    all_to_all x0 -> x1, waiting for transfers between devices: none -> 8.51 us  [body(): along_z = lax.all_to_all(piece, 'z', 0, 0, tiled=True)]
    all_to_all x1, blocking collectives: 25.3 us -> 20.5 us  [body(): arrived = lax.all_to_all(packed, COL, 0, 0, tiled=True)]
    ppermute x1, starting transfers between devices: 8.79 us -> 4.01 us  [body(): got = lax.ppermute(send, 'core', swap)]
    all_to_all x1, blocking collectives: 22.8 us -> 19 us  [body(): pieces = lax.all_to_all(partial, ROW, 0, 0, tiled=True)]
    unnamed x10 -> x4, local copies, waits for them, and re-layouts: 5.05 us -> 1.92 us
  transfers between devices with their start and end apart: 3 -> 3, of which waited for: 3 -> 3; matrix products, arithmetic and copies ran while one was open for 0% -> 0% of each run, Pallas kernels for 0% -> 1%
where the time goes in v2:
time: 120 us; the launch traced here: 119 us
  blocking collectives  73.6 us (61%)
  starting transfers between devices  23.4 us (20%)
  waiting for transfers between devices  13.8 us (12%)
  Pallas kernels  6.54 us (5%)
  local copies, waits for them, and re-layouts  1.92 us (2%)
    all_to_all x1, blocking collectives, body(): own = lax.all_to_all(slabs, ROW, 0, 0, tiled=True)  34.1 us
    all_to_all x1, blocking collectives, body(): arrived = lax.all_to_all(packed, COL, 0, 0, tiled=True)  20.5 us
    all_to_all x1, blocking collectives, body(): pieces = lax.all_to_all(partial, ROW, 0, 0, tiled=True)  19 us
    all_to_all x1, starting transfers between devices, body(): along_z = lax.all_to_all(piece, 'z', 0, 0, tiled=True)  15.8 us
    all_to_all x1, waiting for transfers between devices, body(): along_z = lax.all_to_all(piece, 'z', 0, 0, tiled=True)  8.51 us
    ppermute x1, starting transfers between devices, body(): got = lax.ppermute(send, 'core', swap)  4.01 us
    ppermute x1, waiting for transfers between devices, body(): other = lax.ppermute(own, 'core', swap)  3.76 us
    ppermute x1, starting transfers between devices, body(): other = lax.ppermute(own, 'core', swap)  3.67 us
  transfers between devices with their start and end apart: 3, of which 3 were waited for; matrix products, arithmetic and copies ran while one was open for 0% of the time, Pallas kernels for 1%

profile of v2, /device:TPU:1, one launch (start us, length us, event | category | flops | bytes accessed | tf_op | source)
XLA Modules:
  0.0 119.4 jit_solution(6562291637837530494)
XLA Ops:
  0.0 1.6 %first_density.1 = bf16[16,16,128]{2,1,0:T(8,128)(2,1)} custom-call(bf16[32,1024]{1,0:T(8,128)(2,1)} %den_hbm.1, s32[16,16]{1,0:T(8,128)} %dmask_hbm.1), custom_call_target="tpu_custom_call" | custom-call | tf_op jit(solution)/shard_map/first_density/pallas_call | solution.py:144
  1.6 15.8 %all-to-all-start = ((bf16[16,16,128]{2,1,0:T(8,128)(2,1)}), bf16[16,16,128]{2,1,0:T(8,128)(2,1)S(1)}, u32[]{:S(2)}, u32[]{:S(2)}) async-start(bf16[16,16,128]{2,1,0:T(8,128)(2,1)} %first_density.1), calls=%async_computation | async-start | bytes 131072 | tf_op jit(solution)/shard_map/all_to_all | solution.py:158
  17.4 0.0 copy-start
  17.4 1.2 %copy-done = bf16[8,64,1024]{2,1,0:T(8,128)(2,1)S(1)} copy-done((bf16[8,64,1024]{2,1,0:T(8,128)(2,1)S(1)}, bf16[8,64,1024]{2,1,0:T(8,128)(2,1)}, u32[]{:S(2)}) %copy-start) | copy-done | bytes 1048600
  18.6 0.0 copy-start.1
  18.6 0.7 copy-done.1
  19.3 1.1 prepare.1
  20.4 8.5 %all-to-all-done.den_ref = bf16[16,16,128]{2,1,0:T(8,128)(2,1)S(1)} async-done(((bf16[16,16,128]{2,1,0:T(8,128)(2,1)}), bf16[16,16,128]{2,1,0:T(8,128)(2,1)S(1)}, u32[]{:S(2)}, u32[]{:S(2)}) %all-to-all-start) | async-done | bytes 65568 | tf_op jit(solution)/shard_map/all_to_all | solution.py:158
  28.9 4.0 %collective-permute-start = (bf16[8,64,512]{2,1,0:T(8,128)(2,1)S(1)}, bf16[8,64,512]{2,1,0:T(8,128)(2,1)S(1)}, u32[]{:S(2)}, u32[]{:S(2)}) collective-permute-start(bf16[8,64,512]{2,1,0:T(8,128)(2,1)S(1)} %get-tuple-element.15), channel_id=1, source_target_pairs={{0,1},{1,0},{2,3},{3,2},{4,5},{5,4},{6,7},{7,6},{8,9},{9,8},{10,11... | collective-permute-start | bytes 1572872 | tf_op jit(solution)/shard_map/ppermute | solution.py:170
  32.9 1.5 %collective-permute-done.got_ref = bf16[8,64,512]{2,1,0:T(8,128)(2,1)S(1)} collective-permute-done((bf16[8,64,512]{2,1,0:T(8,128)(2,1)S(1)}, bf16[8,64,512]{2,1,0:T(8,128)(2,1)S(1)}, u32[]{:S(2)}, u32[]{:S(2)}) %collective-permute-start) | collective-permute-done | bytes 524320 | tf_op jit(solution)/shard_map/ppermute | solution.py:170
  34.5 0.3 pack.1
  34.7 34.1 %all_to_all.20.own_ref = bf16[16,128,512]{2,1,0:T(8,128)(2,1)S(1)} all-to-all(bf16[16,128,512]{2,1,0:T(8,128)(2,1)S(1)} %pack.1), channel_id=1, replica_groups=mesh['y'=4,'x'=4,'z'=16,'core'=2] {'y','x'}, dimensions={0} | all-to-all | bytes 4194304 | tf_op jit(solution)/shard_map/all_to_all | solution.py:179
  68.9 3.7 %collective-permute-start.1 = (bf16[16,128,512]{2,1,0:T(8,128)(2,1)S(1)}, bf16[16,128,512]{2,1,0:T(8,128)(2,1)S(1)}, u32[]{:S(2)}, u32[]{:S(2)}) collective-permute-start(bf16[16,128,512]{2,1,0:T(8,128)(2,1)S(1)} %all_to_all.20.own_ref), channel_id=1, source_target_pairs={{0,1},{1,0},{2,3},{3,2},{4,5},{5,4},{6,7},{7,6},{8,9},{9,8},{10,11... | collective-permute-start | bytes 6291464 | tf_op jit(solution)/shard_map/ppermute | solution.py:180
  72.5 3.8 %collective-permute-done.1.other_ref = bf16[16,128,512]{2,1,0:T(8,128)(2,1)S(1)} collective-permute-done((bf16[16,128,512]{2,1,0:T(8,128)(2,1)S(1)}, bf16[16,128,512]{2,1,0:T(8,128)(2,1)S(1)}, u32[]{:S(2)}, u32[]{:S(2)}) %collective-permute-start.1) | collective-permute-done | bytes 2097184 | tf_op jit(solution)/shard_map/ppermute | solution.py:180
  76.3 2.6 %contract.1 = bf16[16,32,1024]{2,1,0:T(8,128)(2,1)S(1)} custom-call(bf16[16,128,512]{2,1,0:T(8,128)(2,1)S(1)} %all_to_all.20.own_ref, bf16[16,128,512]{2,1,0:T(8,128)(2,1)S(1)} %collective-permute-done.1.other_ref), custom_call_target="tpu_custom_call" | custom-call | tf_op jit(solution)/shard_map/contract/pallas_call | solution.py:181
  78.9 19.0 %all_to_all.21.in_ref = bf16[16,32,1024]{2,1,0:T(8,128)(2,1)S(1)} all-to-all(bf16[16,32,1024]{2,1,0:T(8,128)(2,1)S(1)} %contract.1), channel_id=1, replica_groups=mesh['y'=4,'x'=4,'z'=16,'core'=2] {'y','x'}, dimensions={0} | all-to-all | bytes 2097152 | tf_op jit(solution)/shard_map/all_to_all | solution.py:190
  97.9 0.2 sum_aux.1
  98.1 20.5 %all_to_all.22.in_ref = f32[32,8,128]{2,1,0:T(8,128)S(1)} all-to-all(f32[32,8,128]{2,1,0:T(8,128)S(1)} %sum_aux.1), channel_id=1, replica_groups=mesh['y'=4,'x'=4,'z'=16,'core'=2] {'z','core'}, dimensions={0} | all-to-all | bytes 262144 | tf_op jit(solution)/shard_map/all_to_all | solution.py:199
  118.6 0.8 sum_planes.1
Async XLA Ops:
  1.6 27.3 %all-to-all-start = ((bf16[16,16,128]{2,1,0:T(8,128)(2,1)}), bf16[16,16,128]{2,1,0:T(8,128)(2,1)S(1)}, u32[]{:S(2)}, u32[]{:S(2)}) async-start(bf16[16,16,128]{2,1,0:T(8,128)(2,1)} %first_density.1), calls=%async_computation | async-start | bytes 131072 | tf_op jit(solution)/shard_map/all_to_all | solution.py:158
  17.4 1.2 %copy-start = (bf16[8,64,1024]{2,1,0:T(8,128)(2,1)S(1)}, bf16[8,64,1024]{2,1,0:T(8,128)(2,1)}, u32[]{:S(2)}) copy-start(bf16[8,64,1024]{2,1,0:T(8,128)(2,1)} %tc_ref) | copy-start | bytes 3145732
  18.6 0.7 copy-start.1
  28.9 5.5 %collective-permute-start = (bf16[8,64,512]{2,1,0:T(8,128)(2,1)S(1)}, bf16[8,64,512]{2,1,0:T(8,128)(2,1)S(1)}, u32[]{:S(2)}, u32[]{:S(2)}) collective-permute-start(bf16[8,64,512]{2,1,0:T(8,128)(2,1)S(1)} %get-tuple-element.15), channel_id=1, source_target_pairs={{0,1},{1,0},{2,3},{3,2},{4,5},{5,4},{6,7},{7,6},{8,9},{9,8},{10,11... | collective-permute-start | bytes 1572872 | tf_op jit(solution)/shard_map/ppermute | solution.py:170
  68.9 7.4 %collective-permute-start.1 = (bf16[16,128,512]{2,1,0:T(8,128)(2,1)S(1)}, bf16[16,128,512]{2,1,0:T(8,128)(2,1)S(1)}, u32[]{:S(2)}, u32[]{:S(2)}) collective-permute-start(bf16[16,128,512]{2,1,0:T(8,128)(2,1)S(1)} %all_to_all.20.own_ref), channel_id=1, source_target_pairs={{0,1},{1,0},{2,3},{3,2},{4,5},{5,4},{6,7},{7,6},{8,9},{9,8},{10,11... | collective-permute-start | bytes 6291464 | tf_op jit(solution)/shard_map/ppermute | solution.py:180

commit v3 on v2

--- a/solution.py
+++ b/solution.py
@@ -47,7 +47,7 @@
     piece_ref[...] = jnp.broadcast_to(scaled[None], piece_ref.shape)
 
 
-def prepare(tc_ref, pair_ref, keep_ref, send_ref):
+def prepare(tc_ref, pair_ref, keep_ref, send_ref, last_ref):
     row = lax.axis_index("y") * 4 + lax.axis_index("x")
     core = lax.axis_index("core")
     aux, height, basis = tc_ref.shape
@@ -59,6 +59,7 @@
     block = lane // HALF
     hit = src == block * BLK + half * HALF + lane % HALF
     rows = tc_ref[...].reshape(aux * height, basis)
+    most = send_ref.shape[0]
     for tile in range(basis // wide):
         s = [pair_ref[4 * tile + b, row].astype(jnp.float32) for b in range(4)]
         scale = jnp.where(block == 0, s[0], jnp.where(block == 1, s[1], jnp.where(block == 2, s[2], s[3])))
@@ -66,19 +67,27 @@
         out = jnp.dot(rows[:, tile * wide : (tile + 1) * wide], pick, preferred_element_type=jnp.float32)
         out = out.astype(jnp.bfloat16).reshape(aux, height, wide)
         keep_ref[:, :, tile * LANES : (tile + 1) * LANES] = out[:, :, :LANES]
-        send_ref[:, :, tile * LANES : (tile + 1) * LANES] = out[:, :, LANES:]
-
-
-def pack(keep_ref, got_ref, den_ref, out_ref):
+        send_ref[:, :, tile * LANES : (tile + 1) * LANES] = out[:most, :, LANES:]
+        last_ref[:, :, tile * LANES : (tile + 1) * LANES] = out[most:, :, LANES:]
+
+
+def join(keep_ref, got_ref, last_ref, out_ref):
     core = lax.axis_index("core")
-    aux, height, width = keep_ref.shape
-    out_ref[pl.ds(core * aux, aux), :height, :] = keep_ref[...]
-    out_ref[pl.ds((1 - core) * aux, aux), :height, :] = got_ref[...]
+    aux = keep_ref.shape[0]
+    most = got_ref.shape[0] // 2
+    out_ref[pl.ds(core * aux, aux)] = keep_ref[...]
+    out_ref[pl.ds((1 - core) * aux, most)] = got_ref[pl.ds((1 - core) * most, most)]
+    out_ref[pl.ds((1 - core) * aux + most, aux - most)] = last_ref[pl.ds((1 - core) * (aux - most), aux - most)]
+
+
+def pack(slab_ref, den_ref, out_ref):
+    parts, height, width = slab_ref.shape
+    out_ref[:, :height, :] = slab_ref[...]
     groups = width // LANES
     each = den_ref.shape[0] // groups
     for g in range(groups):
         part = den_ref[each * g : each * (g + 1)].reshape(each * PACK, LANES)
-        spread = jnp.broadcast_to(part[None], (2 * aux, each * PACK, LANES))
+        spread = jnp.broadcast_to(part[None], (parts, each * PACK, LANES))
         out_ref[:, height:, g * LANES : (g + 1) * LANES] = spread
 
 
@@ -157,25 +166,35 @@
     piece, three_centre = lax.optimization_barrier((piece, three_centre))
     along_z = lax.all_to_all(piece, "z", 0, 0, tiled=True)
     half = jax.ShapeDtypeStruct((aux, height, width), bf16)
-    keep, send = pl.pallas_call(
+    most = jax.ShapeDtypeStruct((aux - 1, height, width), bf16)
+    last = jax.ShapeDtypeStruct((1, height, width), bf16)
+    keep, send, send_last = pl.pallas_call(
         prepare,
-        out_shape=(half, half),
+        out_shape=(half, most, last),
         in_specs=[vmem(), smem()],
-        out_specs=(vmem(), vmem()),
+        out_specs=(vmem(), vmem(), vmem()),
         compiler_params=pltpu.CompilerParams(vmem_limit_bytes=32 << 20),
         cost_estimate=pl.CostEstimate(flops=4 << 30, bytes_accessed=8 << 20, transcendentals=0),
         name="prepare",
     )(three_centre, pair_mask)
-    along_z, send = lax.optimization_barrier((along_z, send))
-    got = lax.ppermute(send, "core", swap)
+    got = lax.all_gather(send, "core", axis=0, tiled=True)
+    got_last = lax.all_gather(send_last, "core", axis=0, tiled=True)
+    both = pl.pallas_call(
+        join,
+        out_shape=jax.ShapeDtypeStruct((2 * aux, height, width), bf16),
+        in_specs=[vmem()] * 3,
+        out_specs=vmem(),
+        compiler_params=pltpu.CompilerParams(vmem_limit_bytes=32 << 20),
+        name="join",
+    )(keep, got, got_last)
     slabs = pl.pallas_call(
         pack,
         out_shape=jax.ShapeDtypeStruct((2 * aux, 2 * height, width), bf16),
-        in_specs=[vmem()] * 3,
+        in_specs=[vmem()] * 2,
         out_specs=vmem(),
         compiler_params=pltpu.CompilerParams(vmem_limit_bytes=32 << 20),
         name="pack",
-    )(keep, got, along_z)
+    )(both, along_z)
     own = lax.all_to_all(slabs, ROW, 0, 0, tiled=True)
     other = lax.ppermute(own, "core", swap)
     partial = pl.pallas_call(

time: 120 us -> 120 us (level)
  blocking collectives: 73.6 us -> 82.6 us
  waiting for transfers between devices: 13.8 us -> 7.24 us
  starting transfers between devices: 23.4 us -> 20.9 us
    all_to_all x1, waiting for transfers between devices: 8.51 us -> 3.48 us  [body(): along_z = lax.all_to_all(piece, 'z', 0, 0, tiled=True)]
    all_gather x0 -> x2, blocking collectives: none -> 4.95 us  [the longest x1 2.5 us: body(): got_last = lax.all_gather(send_last, 'core', axis=0, tiled=True)]
    all_to_all x1, blocking collectives: 20.5 us -> 25 us  [body(): arrived = lax.all_to_all(packed, COL, 0, 0, tiled=True)]
    ppermute x1 -> x0, starting transfers between devices: 4.01 us -> none  [body(): got = lax.ppermute(send, 'core', swap)]
    ppermute x1 -> x0, waiting for transfers between devices: 1.51 us -> none  [body(): got = lax.ppermute(send, 'core', swap)]
    ppermute x1, starting transfers between devices: 3.67 us -> 5.14 us  [body(): other = lax.ppermute(own, 'core', swap)]
  transfers between devices with their start and end apart: 3 -> 2, of which waited for: 3 -> 2; matrix products, arithmetic and copies ran while one was open for 0% -> 0% of each run, Pallas kernels for 1% -> 1%
where the time goes in v3:
time: 120 us; the launch traced here: 119 us
  blocking collectives  82.6 us (69%)
  starting transfers between devices  20.9 us (17%)
  waiting for transfers between devices  7.24 us (6%)
  Pallas kernels  6.6 us (6%)
  local copies, waits for them, and re-layouts  1.92 us (2%)
    all_to_all x1, blocking collectives, body(): own = lax.all_to_all(slabs, ROW, 0, 0, tiled=True)  33.7 us
    all_to_all x1, blocking collectives, body(): arrived = lax.all_to_all(packed, COL, 0, 0, tiled=True)  25 us
    all_to_all x1, blocking collectives, body(): pieces = lax.all_to_all(partial, ROW, 0, 0, tiled=True)  19 us
    all_to_all x1, starting transfers between devices, body(): along_z = lax.all_to_all(piece, 'z', 0, 0, tiled=True)  15.8 us
    ppermute x1, starting transfers between devices, body(): other = lax.ppermute(own, 'core', swap)  5.14 us
    ppermute x1, waiting for transfers between devices, body(): other = lax.ppermute(own, 'core', swap)  3.76 us
    all_to_all x1, waiting for transfers between devices, body(): along_z = lax.all_to_all(piece, 'z', 0, 0, tiled=True)  3.48 us
    pallas_call x1, Pallas kernels, body(): pl.pallas_call(contract, out_shape=jax.ShapeDtypeStruct((2 * aux, HALF, b...  2.57 us
  transfers between devices with their start and end apart: 2, of which 2 were waited for; matrix products, arithmetic and copies ran while one was open for 0% of the time, Pallas kernels for 1%

profile of v3, /device:TPU:1, one launch (start us, length us, event | category | flops | bytes accessed | tf_op | source)
XLA Modules:
  0.0 119.4 jit_solution(1938706177265669489)
XLA Ops:
  0.0 1.6 %first_density.1 = bf16[16,16,128]{2,1,0:T(8,128)(2,1)} custom-call(bf16[32,1024]{1,0:T(8,128)(2,1)} %den_hbm.1, s32[16,16]{1,0:T(8,128)} %dmask_hbm.1), custom_call_target="tpu_custom_call" | custom-call | tf_op jit(solution)/shard_map/first_density/pallas_call | solution.py:153
  1.6 15.8 %all-to-all-start = ((bf16[16,16,128]{2,1,0:T(8,128)(2,1)}), bf16[16,16,128]{2,1,0:T(8,128)(2,1)S(1)}, u32[]{:S(2)}, u32[]{:S(2)}) async-start(bf16[16,16,128]{2,1,0:T(8,128)(2,1)} %first_density.1), calls=%async_computation | async-start | bytes 131072 | tf_op jit(solution)/shard_map/all_to_all | solution.py:167
  17.3 0.0 copy-start
  17.4 1.2 %copy-done = bf16[8,64,1024]{2,1,0:T(8,128)(2,1)S(1)} copy-done((bf16[8,64,1024]{2,1,0:T(8,128)(2,1)S(1)}, bf16[8,64,1024]{2,1,0:T(8,128)(2,1)}, u32[]{:S(2)}) %copy-start) | copy-done | bytes 1048600
  18.6 0.0 copy-start.1
  18.6 0.7 copy-done.1
  19.3 1.1 prepare.1
  20.4 2.5 %all_gather.7.last_ref = bf16[2,64,512]{2,1,0:T(8,128)(2,1)S(1)} all-gather(bf16[1,64,512]{2,1,0:T(8,128)(2,1)S(1)} %get-tuple-element.13), channel_id=1, replica_groups=mesh['y'=4,'x'=4,'z'=16,'core'=2] {'core'}, dimensions={0}, use_global_device_ids=true | all-gather | bytes 196608 | tf_op jit(solution)/shard_map/all_gather | solution.py:181
  22.9 2.4 %all_gather.6.got_ref = bf16[14,64,512]{2,1,0:T(8,128)(2,1)S(1)} all-gather(bf16[7,64,512]{2,1,0:T(8,128)(2,1)S(1)} %get-tuple-element.12), channel_id=1, replica_groups=mesh['y'=4,'x'=4,'z'=16,'core'=2] {'core'}, dimensions={0}, use_global_device_ids=true | all-gather | bytes 1376256 | tf_op jit(solution)/shard_map/all_gather | solution.py:180
  25.4 0.1 join.1.slab_ref
  25.4 3.5 %all-to-all-done.den_ref = bf16[16,16,128]{2,1,0:T(8,128)(2,1)S(1)} async-done(((bf16[16,16,128]{2,1,0:T(8,128)(2,1)}), bf16[16,16,128]{2,1,0:T(8,128)(2,1)S(1)}, u32[]{:S(2)}, u32[]{:S(2)}) %all-to-all-start) | async-done | bytes 65568 | tf_op jit(solution)/shard_map/all_to_all | solution.py:167
  28.9 0.3 pack.1
  29.2 33.7 %all_to_all.20.own_ref = bf16[16,128,512]{2,1,0:T(8,128)(2,1)S(1)} all-to-all(bf16[16,128,512]{2,1,0:T(8,128)(2,1)S(1)} %pack.1), channel_id=1, replica_groups=mesh['y'=4,'x'=4,'z'=16,'core'=2] {'y','x'}, dimensions={0} | all-to-all | bytes 4194304 | tf_op jit(solution)/shard_map/all_to_all | solution.py:198
  62.9 5.1 %collective-permute-start = (bf16[16,128,512]{2,1,0:T(8,128)(2,1)S(1)}, bf16[16,128,512]{2,1,0:T(8,128)(2,1)S(1)}, u32[]{:S(2)}, u32[]{:S(2)}) collective-permute-start(bf16[16,128,512]{2,1,0:T(8,128)(2,1)S(1)} %all_to_all.20.own_ref), channel_id=1, source_target_pairs={{0,1},{1,0},{2,3},{3,2},{4,5},{5,4},{6,7},{7,6},{8,9},{9,8},{10,11... | collective-permute-start | bytes 6291464 | tf_op jit(solution)/shard_map/ppermute | solution.py:199
  68.0 3.8 %collective-permute-done.other_ref = bf16[16,128,512]{2,1,0:T(8,128)(2,1)S(1)} collective-permute-done((bf16[16,128,512]{2,1,0:T(8,128)(2,1)S(1)}, bf16[16,128,512]{2,1,0:T(8,128)(2,1)S(1)}, u32[]{:S(2)}, u32[]{:S(2)}) %collective-permute-start) | collective-permute-done | bytes 2097184 | tf_op jit(solution)/shard_map/ppermute | solution.py:199
  71.8 2.6 %contract.1 = bf16[16,32,1024]{2,1,0:T(8,128)(2,1)S(1)} custom-call(bf16[16,128,512]{2,1,0:T(8,128)(2,1)S(1)} %all_to_all.20.own_ref, bf16[16,128,512]{2,1,0:T(8,128)(2,1)S(1)} %collective-permute-done.other_ref), custom_call_target="tpu_custom_call" | custom-call | tf_op jit(solution)/shard_map/contract/pallas_call | solution.py:200
  74.3 19.0 %all_to_all.21.in_ref = bf16[16,32,1024]{2,1,0:T(8,128)(2,1)S(1)} all-to-all(bf16[16,32,1024]{2,1,0:T(8,128)(2,1)S(1)} %contract.1), channel_id=1, replica_groups=mesh['y'=4,'x'=4,'z'=16,'core'=2] {'y','x'}, dimensions={0} | all-to-all | bytes 2097152 | tf_op jit(solution)/shard_map/all_to_all | solution.py:209
  93.4 0.2 sum_aux.1
  93.6 25.0 %all_to_all.22.in_ref = f32[32,8,128]{2,1,0:T(8,128)S(1)} all-to-all(f32[32,8,128]{2,1,0:T(8,128)S(1)} %sum_aux.1), channel_id=1, replica_groups=mesh['y'=4,'x'=4,'z'=16,'core'=2] {'z','core'}, dimensions={0} | all-to-all | bytes 262144 | tf_op jit(solution)/shard_map/all_to_all | solution.py:218
  118.6 0.8 sum_planes.1
Async XLA Ops:
  1.6 27.3 %all-to-all-start = ((bf16[16,16,128]{2,1,0:T(8,128)(2,1)}), bf16[16,16,128]{2,1,0:T(8,128)(2,1)S(1)}, u32[]{:S(2)}, u32[]{:S(2)}) async-start(bf16[16,16,128]{2,1,0:T(8,128)(2,1)} %first_density.1), calls=%async_computation | async-start | bytes 131072 | tf_op jit(solution)/shard_map/all_to_all | solution.py:167
  17.3 1.2 %copy-start = (bf16[8,64,1024]{2,1,0:T(8,128)(2,1)S(1)}, bf16[8,64,1024]{2,1,0:T(8,128)(2,1)}, u32[]{:S(2)}) copy-start(bf16[8,64,1024]{2,1,0:T(8,128)(2,1)} %tc_ref) | copy-start | bytes 3145732
  18.6 0.7 copy-start.1
  62.9 8.9 %collective-permute-start = (bf16[16,128,512]{2,1,0:T(8,128)(2,1)S(1)}, bf16[16,128,512]{2,1,0:T(8,128)(2,1)S(1)}, u32[]{:S(2)}, u32[]{:S(2)}) collective-permute-start(bf16[16,128,512]{2,1,0:T(8,128)(2,1)S(1)} %all_to_all.20.own_ref), channel_id=1, source_target_pairs={{0,1},{1,0},{2,3},{3,2},{4,5},{5,4},{6,7},{7,6},{8,9},{9,8},{10,11... | collective-permute-start | bytes 6291464 | tf_op jit(solution)/shard_map/ppermute | solution.py:199

commit v4 on v3

--- a/solution.py
+++ b/solution.py
@@ -15,6 +15,10 @@
 HALF = 32
 LANES = 128
 PACK = 16
+PLANES = 16
+TURN = PLANES // 2
+ROWS = 16
+SHIFT = 10
 
 
 def vmem():
@@ -86,7 +90,8 @@
     groups = width // LANES
     each = den_ref.shape[0] // groups
     for g in range(groups):
-        part = den_ref[each * g : each * (g + 1)].reshape(each * PACK, LANES)
+        slot = (each * g + TURN) % PLANES
+        part = den_ref[slot : slot + each].reshape(each * PACK, LANES)
         spread = jnp.broadcast_to(part[None], (parts, each * PACK, LANES))
         out_ref[:, height:, g * LANES : (g + 1) * LANES] = spread
 
@@ -99,22 +104,32 @@
     groups = width // LANES
     each = den.shape[0] // groups
     for ref, side in ((own_ref, core), (other_ref, 1 - core)):
-        for k in range(2 * tiles):
-            cols = slice(k % tiles * LANES, (k % tiles + 1) * LANES)
+        for k in range(ROWS):
+            row = (k + SHIFT) % ROWS
+            cols = slice(row % tiles * LANES, (row % tiles + 1) * LANES)
             for g in range(groups):
                 part = ref[k, height:, g * LANES : (g + 1) * LANES].reshape(each, PACK, LANES)
-                den[each * g : each * (g + 1), side, k // tiles, :, cols] = part
-    own = own_ref[:, :height, :].reshape(parts * height, width)
+                den[each * g : each * (g + 1), side, row // tiles, :, cols] = part
+
+    def slab(ref):
+        turned = jnp.concatenate([ref[ROWS - SHIFT :, :height, :], ref[: ROWS - SHIFT, :height, :]])
+        return turned.reshape(parts * height, width)
+
+    def put(value, cols):
+        value = value.astype(jnp.bfloat16).reshape(ROWS, out_ref.shape[1], width)
+        out_ref[: ROWS - SHIFT, :, cols] = value[SHIFT:]
+        out_ref[ROWS - SHIFT :, :, cols] = value[:SHIFT]
+
+    own = slab(own_ref)
     density = den[...].reshape(parts * height, den.shape[-1])
     built = lax.dot_general(
         own, density, (((0,), (0,)), ((), ())), preferred_element_type=jnp.float32
     ).astype(jnp.bfloat16)
-    other = other_ref[:, :height, :].reshape(parts * height, width)
-    shape = (out_ref.shape[0], out_ref.shape[1], width)
-    mine = jnp.dot(built, own, preferred_element_type=jnp.float32).astype(jnp.bfloat16)
-    out_ref[:, :, pl.ds(pl.multiple_of(core * width, LANES), width)] = mine.reshape(shape)
-    theirs = jnp.dot(built, other, preferred_element_type=jnp.float32).astype(jnp.bfloat16)
-    out_ref[:, :, pl.ds(pl.multiple_of((1 - core) * width, LANES), width)] = theirs.reshape(shape)
+    put(jnp.dot(built, own, preferred_element_type=jnp.float32), pl.ds(pl.multiple_of(core * width, LANES), width))
+    put(
+        jnp.dot(built, slab(other_ref), preferred_element_type=jnp.float32),
+        pl.ds(pl.multiple_of((1 - core) * width, LANES), width),
+    )
 
 
 def gather_groups(groups, start):
@@ -130,7 +145,7 @@
             total = total + in_ref[k, :, cols].astype(jnp.float32)
         groups = [total[8 * g : 8 * g + 8] for g in range(4)]
         for q in range(4):
-            dest = ((tile % 4) * 4 + q) * 2 + tile // 4
+            dest = ((tile % 4 * 4 + q + TURN) % PLANES) * 2 + tile // 4
             out_ref[dest] = gather_groups(groups, q * HALF)
 
 
@@ -149,7 +164,7 @@
     width = basis // 2
     bf16, f32 = jnp.bfloat16, jnp.float32
     swap = [(0, 1), (1, 0)]
-    planes = 16
+    planes = PLANES
     piece = pl.pallas_call(
         first_density,
         out_shape=jax.ShapeDtypeStruct((planes, PACK, LANES), bf16),
@@ -164,7 +179,8 @@
         name="first_density",
     )(density, density_mask)
     piece, three_centre = lax.optimization_barrier((piece, three_centre))
-    along_z = lax.all_to_all(piece, "z", 0, 0, tiled=True)
+    turned = [(i + TURN) % PLANES for i in range(PLANES)]
+    along_z = lax.all_to_all(piece, "z", 0, 0, axis_index_groups=[turned], tiled=True)
     half = jax.ShapeDtypeStruct((aux, height, width), bf16)
     most = jax.ShapeDtypeStruct((aux - 1, height, width), bf16)
     last = jax.ShapeDtypeStruct((1, height, width), bf16)
@@ -195,7 +211,8 @@
         compiler_params=pltpu.CompilerParams(vmem_limit_bytes=32 << 20),
         name="pack",
     )(both, along_z)
-    own = lax.all_to_all(slabs, ROW, 0, 0, tiled=True)
+    from_corner = [[(i + SHIFT) % ROWS for i in range(ROWS)]]
+    own = lax.all_to_all(slabs, ROW, 0, 0, axis_index_groups=from_corner, tiled=True)
     other = lax.ppermute(own, "core", swap)
     partial = pl.pallas_call(
         contract,
@@ -206,7 +223,7 @@
         compiler_params=pltpu.CompilerParams(vmem_limit_bytes=40 << 20),
         name="contract",
     )(own, other)
-    pieces = lax.all_to_all(partial, ROW, 0, 0, tiled=True)
+    pieces = lax.all_to_all(partial, ROW, 0, 0, axis_index_groups=from_corner, tiled=True)
     packed = pl.pallas_call(
         sum_aux,
         out_shape=jax.ShapeDtypeStruct((32, 8, LANES), f32),
@@ -215,7 +232,8 @@
         compiler_params=pltpu.CompilerParams(vmem_limit_bytes=16 << 20),
         name="sum_aux",
     )(pieces)
-    arrived = lax.all_to_all(packed, COL, 0, 0, tiled=True)
+    pairs = [[2 * z + c for z in turned for c in range(2)]]
+    arrived = lax.all_to_all(packed, COL, 0, 0, axis_index_groups=pairs, tiled=True)
     return pl.pallas_call(
         sum_planes,
         out_shape=jax.ShapeDtypeStruct((HALF, BLK), f32),

time: 120 us -> 110 us (0.917)
  blocking collectives: 82.6 us -> 75.8 us
  waiting for transfers between devices: 7.24 us -> 3.77 us
    all_to_all x3, blocking collectives: 77.7 us -> 70.5 us  [the longest x1 31.8 us: body(): lax.all_to_all(slabs, ROW, 0, 0, axis_index_groups=from_corner, tiled=True)]
    all_to_all x1, waiting for transfers between devices: 3.48 us -> 0.01 us  [body(): lax.all_to_all(piece, 'z', 0, 0, axis_index_groups=[turned], tiled=True)]
    all_to_all x1, starting transfers between devices: 15.8 us -> 19.1 us  [body(): lax.all_to_all(piece, 'z', 0, 0, axis_index_groups=[turned], tiled=True)]
    ppermute x1, starting transfers between devices: 5.14 us -> 2.74 us  [body(): other = lax.ppermute(own, 'core', swap)]
  transfers between devices with their start and end apart: 2 -> 2, of which waited for: 2 -> 1; matrix products, arithmetic and copies ran while one was open for 0% -> 0% of each run, Pallas kernels for 1% -> 1%
where the time goes in v4:
time: 110 us
  blocking collectives  75.8 us (69%)
  starting transfers between devices  21.9 us (20%)
  Pallas kernels  6.62 us (6%)
  waiting for transfers between devices  3.77 us (3%)
  local copies, waits for them, and re-layouts  1.92 us (2%)
    all_to_all x1, blocking collectives, body(): lax.all_to_all(slabs, ROW, 0, 0, axis_index_groups=from_corner, tiled=True)  31.8 us
    all_to_all x1, blocking collectives, body(): lax.all_to_all(packed, COL, 0, 0, axis_index_groups=pairs, tiled=True)  19.4 us
    all_to_all x1, blocking collectives, body(): lax.all_to_all(partial, ROW, 0, 0, axis_index_groups=from_corner, tiled=T...  19.3 us
    all_to_all x1, starting transfers between devices, body(): lax.all_to_all(piece, 'z', 0, 0, axis_index_groups=[turned], tiled=True)  19.1 us
    ppermute x1, waiting for transfers between devices, body(): other = lax.ppermute(own, 'core', swap)  3.76 us
    all_gather x1, blocking collectives, body(): got_last = lax.all_gather(send_last, 'core', axis=0, tiled=True)  2.78 us
    ppermute x1, starting transfers between devices, body(): other = lax.ppermute(own, 'core', swap)  2.74 us
    pallas_call x1, Pallas kernels, body(): pl.pallas_call(contract, out_shape=jax.ShapeDtypeStruct((2 * aux, HALF, b...  2.6 us
  transfers between devices with their start and end apart: 2, of which 1 were waited for; matrix products, arithmetic and copies ran while one was open for 0% of the time, Pallas kernels for 1%

profile of v4, /device:TPU:1, one launch (start us, length us, event | category | flops | bytes accessed | tf_op | source)
XLA Modules:
  0.0 110.0 jit_solution(3024124429906609570)
XLA Ops:
  0.0 1.6 %first_density.1 = bf16[16,16,128]{2,1,0:T(8,128)(2,1)} custom-call(bf16[32,1024]{1,0:T(8,128)(2,1)} %den_hbm.1, s32[16,16]{1,0:T(8,128)} %dmask_hbm.1), custom_call_target="tpu_custom_call" | custom-call | tf_op jit(solution)/shard_map/first_density/pallas_call | solution.py:168
  1.6 19.1 %all-to-all-start = ((bf16[16,16,128]{2,1,0:T(8,128)(2,1)}), bf16[16,16,128]{2,1,0:T(8,128)(2,1)S(1)}, u32[]{:S(2)}, u32[]{:S(2)}) async-start(bf16[16,16,128]{2,1,0:T(8,128)(2,1)} %first_density.1), calls=%async_computation | async-start | bytes 131072 | tf_op jit(solution)/shard_map/all_to_all | solution.py:183
  20.7 0.0 copy-start
  20.7 1.2 %copy-done = bf16[8,64,1024]{2,1,0:T(8,128)(2,1)S(1)} copy-done((bf16[8,64,1024]{2,1,0:T(8,128)(2,1)S(1)}, bf16[8,64,1024]{2,1,0:T(8,128)(2,1)}, u32[]{:S(2)}) %copy-start) | copy-done | bytes 1048600
  21.9 0.0 copy-start.1
  21.9 0.7 copy-done.1
  22.6 1.1 %prepare.1 = (bf16[8,64,512]{2,1,0:T(8,128)(2,1)S(1)}, bf16[7,64,512]{2,1,0:T(8,128)(2,1)S(1)}, bf16[1,64,512]{2,1,0:T(8,128)(2,1)S(1)}) custom-call(bf16[8,64,1024]{2,1,0:T(8,128)(2,1)S(1)} %copy-done, s32[16,16]{1,0:T(8,128)S(1)} %copy-done.1), custom_call_target="tpu_custom_call" | custom-call | flops 4294967296 | bytes 8388608 | tf_op jit(solution)/shard_map/prepare/pallas_call | solution.py:187
  23.8 2.8 %all_gather.7.last_ref = bf16[2,64,512]{2,1,0:T(8,128)(2,1)S(1)} all-gather(bf16[1,64,512]{2,1,0:T(8,128)(2,1)S(1)} %get-tuple-element.13), channel_id=1, replica_groups=mesh['y'=4,'x'=4,'z'=16,'core'=2] {'core'}, dimensions={0}, use_global_device_ids=true | all-gather | bytes 196608 | tf_op jit(solution)/shard_map/all_gather | solution.py:197
  26.6 2.4 %all_gather.6.got_ref = bf16[14,64,512]{2,1,0:T(8,128)(2,1)S(1)} all-gather(bf16[7,64,512]{2,1,0:T(8,128)(2,1)S(1)} %get-tuple-element.12), channel_id=1, replica_groups=mesh['y'=4,'x'=4,'z'=16,'core'=2] {'core'}, dimensions={0}, use_global_device_ids=true | all-gather | bytes 1376256 | tf_op jit(solution)/shard_map/all_gather | solution.py:196
  29.0 0.1 join.1.slab_ref
  29.1 0.0 all-to-all-done.den_ref
  29.1 0.3 pack.1
  29.4 31.8 %all_to_all.20.own_ref = bf16[16,128,512]{2,1,0:T(8,128)(2,1)S(1)} all-to-all(bf16[16,128,512]{2,1,0:T(8,128)(2,1)S(1)} %pack.1), channel_id=1, replica_groups={{320,352,384,416,448,480,0,32,64,96,128,160,192,224,256,288},{321,353,3..., dimensions={0} | all-to-all | bytes 4194304 | tf_op jit(solution)/shard_map/all_to_all | solution.py:215
  61.2 2.7 %collective-permute-start = (bf16[16,128,512]{2,1,0:T(8,128)(2,1)S(1)}, bf16[16,128,512]{2,1,0:T(8,128)(2,1)S(1)}, u32[]{:S(2)}, u32[]{:S(2)}) collective-permute-start(bf16[16,128,512]{2,1,0:T(8,128)(2,1)S(1)} %all_to_all.20.own_ref), channel_id=1, source_target_pairs={{0,1},{1,0},{2,3},{3,2},{4,5},{5,4},{6,7},{7,6},{8,9},{9,8},{10,11... | collective-permute-start | bytes 6291464 | tf_op jit(solution)/shard_map/ppermute | solution.py:216
  64.0 3.8 %collective-permute-done.other_ref = bf16[16,128,512]{2,1,0:T(8,128)(2,1)S(1)} collective-permute-done((bf16[16,128,512]{2,1,0:T(8,128)(2,1)S(1)}, bf16[16,128,512]{2,1,0:T(8,128)(2,1)S(1)}, u32[]{:S(2)}, u32[]{:S(2)}) %collective-permute-start) | collective-permute-done | bytes 2097184 | tf_op jit(solution)/shard_map/ppermute | solution.py:216
  67.7 2.6 %contract.1 = bf16[16,32,1024]{2,1,0:T(8,128)(2,1)S(1)} custom-call(bf16[16,128,512]{2,1,0:T(8,128)(2,1)S(1)} %all_to_all.20.own_ref, bf16[16,128,512]{2,1,0:T(8,128)(2,1)S(1)} %collective-permute-done.other_ref), custom_call_target="tpu_custom_call" | custom-call | tf_op jit(solution)/shard_map/contract/pallas_call | solution.py:217
  70.3 19.3 %all_to_all.21.in_ref = bf16[16,32,1024]{2,1,0:T(8,128)(2,1)S(1)} all-to-all(bf16[16,32,1024]{2,1,0:T(8,128)(2,1)S(1)} %contract.1), channel_id=1, replica_groups={{320,352,384,416,448,480,0,32,64,96,128,160,192,224,256,288},{321,353,3..., dimensions={0} | all-to-all | bytes 2097152 | tf_op jit(solution)/shard_map/all_to_all | solution.py:226
  89.6 0.2 sum_aux.1
  89.8 19.4 %all_to_all.22.in_ref = f32[32,8,128]{2,1,0:T(8,128)S(1)} all-to-all(f32[32,8,128]{2,1,0:T(8,128)S(1)} %sum_aux.1), channel_id=1, replica_groups={{16,17,18,19,20,21,22,23,24,25,26,27,28,29,30,31,0,1,2,3,4,5,6,7,8,9,10..., dimensions={0} | all-to-all | bytes 262144 | tf_op jit(solution)/shard_map/all_to_all | solution.py:236
  109.2 0.8 sum_planes.1
Async XLA Ops:
  1.6 27.5 %all-to-all-start = ((bf16[16,16,128]{2,1,0:T(8,128)(2,1)}), bf16[16,16,128]{2,1,0:T(8,128)(2,1)S(1)}, u32[]{:S(2)}, u32[]{:S(2)}) async-start(bf16[16,16,128]{2,1,0:T(8,128)(2,1)} %first_density.1), calls=%async_computation | async-start | bytes 131072 | tf_op jit(solution)/shard_map/all_to_all | solution.py:183
  20.7 1.2 %copy-start = (bf16[8,64,1024]{2,1,0:T(8,128)(2,1)S(1)}, bf16[8,64,1024]{2,1,0:T(8,128)(2,1)}, u32[]{:S(2)}) copy-start(bf16[8,64,1024]{2,1,0:T(8,128)(2,1)} %tc_ref) | copy-start | bytes 3145732
  21.9 0.7 copy-start.1
  61.2 6.5 %collective-permute-start = (bf16[16,128,512]{2,1,0:T(8,128)(2,1)S(1)}, bf16[16,128,512]{2,1,0:T(8,128)(2,1)S(1)}, u32[]{:S(2)}, u32[]{:S(2)}) collective-permute-start(bf16[16,128,512]{2,1,0:T(8,128)(2,1)S(1)} %all_to_all.20.own_ref), channel_id=1, source_target_pairs={{0,1},{1,0},{2,3},{3,2},{4,5},{5,4},{6,7},{7,6},{8,9},{9,8},{10,11... | collective-permute-start | bytes 6291464 | tf_op jit(solution)/shard_map/ppermute | solution.py:216

commit v5 on v4

--- a/solution.py
+++ b/solution.py
@@ -29,32 +29,23 @@
     return pl.BlockSpec(memory_space=SMEM)
 
 
-def first_density(den_hbm, dmask_hbm, piece_ref, den, dmask, sems):
+def prepare(
+    tc_hbm, den_hbm, pair_hbm, dmask_hbm, piece_ref, keep_ref, send_ref, last_ref, tc, den, pair, dmask, sems
+):
     row = lax.axis_index("y") * 4 + lax.axis_index("x")
-    tiles = den_hbm.shape[1] // LANES
+    core = lax.axis_index("core")
+    aux, height, basis = tc.shape
+    tiles = basis // LANES
     tile = row % tiles
     part = row // tiles
-    source = den_hbm.at[
+    piece = den_hbm.at[
         pl.ds(pl.multiple_of(part * PACK, PACK), PACK), pl.ds(pl.multiple_of(tile * LANES, LANES), LANES)
     ]
-    fetch_den = pltpu.make_async_copy(source, den, sems.at[0])
-    fetch_mask = pltpu.make_async_copy(dmask_hbm, dmask, sems.at[1])
-    fetch_den.start()
-    fetch_mask.start()
-    fetch_mask.wait()
-    fetch_den.wait()
-    low = lax.broadcasted_iota(jnp.int32, (PACK, LANES), 1) < BLK
-    mask_row = lax.axis_index("z")
-    a = dmask[mask_row, 2 * tile].astype(jnp.float32)
-    b = dmask[mask_row, 2 * tile + 1].astype(jnp.float32)
-    scaled = (den[...].astype(jnp.float32) * jnp.where(low, a, b)).astype(jnp.bfloat16)
-    piece_ref[...] = jnp.broadcast_to(scaled[None], piece_ref.shape)
-
-
-def prepare(tc_ref, pair_ref, keep_ref, send_ref, last_ref):
-    row = lax.axis_index("y") * 4 + lax.axis_index("x")
-    core = lax.axis_index("core")
-    aux, height, basis = tc_ref.shape
+    moves = [(pair_hbm, pair), (dmask_hbm, dmask), (piece, den)]
+    moves += [(tc_hbm.at[k], tc.at[k]) for k in range(aux)]
+    copies = [pltpu.make_async_copy(src, dst, sems.at[k]) for k, (src, dst) in enumerate(moves)]
+    for copy in copies:
+        copy.start()
     wide = 2 * LANES
     src = lax.broadcasted_iota(jnp.int32, (wide, wide), 0)
     dst = lax.broadcasted_iota(jnp.int32, (wide, wide), 1)
@@ -62,17 +53,34 @@
     lane = dst % LANES
     block = lane // HALF
     hit = src == block * BLK + half * HALF + lane % HALF
-    rows = tc_ref[...].reshape(aux * height, basis)
+    for copy in copies[:3]:
+        copy.wait()
+    low = lax.broadcasted_iota(jnp.int32, (PACK, LANES), 1) < BLK
+    mask_row = lax.axis_index("z")
+    a = dmask[mask_row, 2 * tile].astype(jnp.float32)
+    b = dmask[mask_row, 2 * tile + 1].astype(jnp.float32)
+    scaled = (den[...].astype(jnp.float32) * jnp.where(low, a, b)).astype(jnp.bfloat16)
+    piece_ref[...] = jnp.broadcast_to(scaled[None], piece_ref.shape)
+    picks = []
+    for t in range(basis // wide):
+        s = [pair[4 * t + b, row].astype(jnp.float32) for b in range(4)]
+        scale = jnp.where(block == 0, s[0], jnp.where(block == 1, s[1], jnp.where(block == 2, s[2], s[3])))
+        picks.append(jnp.where(hit, scale, 0.0).astype(jnp.bfloat16))
     most = send_ref.shape[0]
-    for tile in range(basis // wide):
-        s = [pair_ref[4 * tile + b, row].astype(jnp.float32) for b in range(4)]
-        scale = jnp.where(block == 0, s[0], jnp.where(block == 1, s[1], jnp.where(block == 2, s[2], s[3])))
-        pick = jnp.where(hit, scale, 0.0).astype(jnp.bfloat16)
-        out = jnp.dot(rows[:, tile * wide : (tile + 1) * wide], pick, preferred_element_type=jnp.float32)
-        out = out.astype(jnp.bfloat16).reshape(aux, height, wide)
-        keep_ref[:, :, tile * LANES : (tile + 1) * LANES] = out[:, :, :LANES]
-        send_ref[:, :, tile * LANES : (tile + 1) * LANES] = out[:most, :, LANES:]
-        last_ref[:, :, tile * LANES : (tile + 1) * LANES] = out[most:, :, LANES:]
+    step = 2
+    for k in range(0, aux, step):
+        for copy in copies[3 + k : 3 + k + step]:
+            copy.wait()
+        rows = tc[k : k + step].reshape(step * height, basis)
+        for t, pick in enumerate(picks):
+            cols = slice(t * LANES, (t + 1) * LANES)
+            out = jnp.dot(rows[:, t * wide : (t + 1) * wide], pick, preferred_element_type=jnp.float32)
+            out = out.astype(jnp.bfloat16).reshape(step, height, wide)
+            keep_ref[k : k + step, :, cols] = out[:, :, :LANES]
+            inside = min(step, most - k)
+            send_ref[k : k + inside, :, cols] = out[:inside, :, LANES:]
+            if inside < step:
+                last_ref[:, :, cols] = out[inside:, :, LANES:]
 
 
 def join(keep_ref, got_ref, last_ref, out_ref):
@@ -165,34 +173,26 @@
     bf16, f32 = jnp.bfloat16, jnp.float32
     swap = [(0, 1), (1, 0)]
     planes = PLANES
-    piece = pl.pallas_call(
-        first_density,
-        out_shape=jax.ShapeDtypeStruct((planes, PACK, LANES), bf16),
-        in_specs=[pl.BlockSpec(memory_space=pltpu.HBM)] * 2,
-        out_specs=vmem(),
-        scratch_shapes=[
-            VMEM((PACK, LANES), bf16),
-            SMEM(density_mask.shape, jnp.int32),
-            pltpu.SemaphoreType.DMA((2,)),
-        ],
-        compiler_params=pltpu.CompilerParams(vmem_limit_bytes=60 << 20),
-        name="first_density",
-    )(density, density_mask)
-    piece, three_centre = lax.optimization_barrier((piece, three_centre))
-    turned = [(i + TURN) % PLANES for i in range(PLANES)]
-    along_z = lax.all_to_all(piece, "z", 0, 0, axis_index_groups=[turned], tiled=True)
     half = jax.ShapeDtypeStruct((aux, height, width), bf16)
     most = jax.ShapeDtypeStruct((aux - 1, height, width), bf16)
     last = jax.ShapeDtypeStruct((1, height, width), bf16)
-    keep, send, send_last = pl.pallas_call(
+    piece, keep, send, send_last = pl.pallas_call(
         prepare,
-        out_shape=(half, most, last),
-        in_specs=[vmem(), smem()],
-        out_specs=(vmem(), vmem(), vmem()),
-        compiler_params=pltpu.CompilerParams(vmem_limit_bytes=32 << 20),
-        cost_estimate=pl.CostEstimate(flops=4 << 30, bytes_accessed=8 << 20, transcendentals=0),
+        out_shape=(jax.ShapeDtypeStruct((planes, PACK, LANES), bf16), half, most, last),
+        in_specs=[pl.BlockSpec(memory_space=pltpu.HBM)] * 4,
+        out_specs=(vmem(),) * 4,
+        scratch_shapes=[
+            VMEM(three_centre.shape, bf16),
+            VMEM((PACK, LANES), bf16),
+            SMEM(pair_mask.shape, jnp.int32),
+            SMEM(density_mask.shape, jnp.int32),
+            pltpu.SemaphoreType.DMA((3 + aux,)),
+        ],
+        compiler_params=pltpu.CompilerParams(vmem_limit_bytes=40 << 20),
         name="prepare",
-    )(three_centre, pair_mask)
+    )(*(pltpu.with_memory_space_constraint(a, pltpu.HBM) for a in (three_centre, density, pair_mask, density_mask)))
+    turned = [(i + TURN) % PLANES for i in range(PLANES)]
+    along_z = lax.all_to_all(piece, "z", 0, 0, axis_index_groups=[turned], tiled=True)
     got = lax.all_gather(send, "core", axis=0, tiled=True)
     got_last = lax.all_gather(send_last, "core", axis=0, tiled=True)
     both = pl.pallas_call(

time: 110 us -> 108 us (0.982)
  local copies, waits for them, and re-layouts: 1.92 us -> 0 us
    unnamed x4 -> x0, local copies, waits for them, and re-layouts: 1.92 us -> none
    pallas_call x2 -> x1, Pallas kernels: 2.7 us -> 2.41 us  [body(): pl.pallas_call(prepare, out_shape=(jax.ShapeDtypeStruct((planes, PACK, LA...]
  transfers between devices with their start and end apart: 2 -> 2, of which waited for: 1 -> 1; matrix products, arithmetic and copies ran while one was open for 0% -> 0% of each run, Pallas kernels for 1% -> 0%
where the time goes in v5:
time: 108 us
  blocking collectives  75.7 us (70%)
  starting transfers between devices  21.9 us (20%)
  Pallas kernels  6.34 us (6%)
  waiting for transfers between devices  3.77 us (3%)
    all_to_all x1, blocking collectives, body(): lax.all_to_all(slabs, ROW, 0, 0, axis_index_groups=from_corner, tiled=True)  31.8 us
    all_to_all x1, blocking collectives, body(): lax.all_to_all(packed, COL, 0, 0, axis_index_groups=pairs, tiled=True)  19.4 us
    all_to_all x1, blocking collectives, body(): lax.all_to_all(partial, ROW, 0, 0, axis_index_groups=from_corner, tiled=T...  19.3 us
    all_to_all x1, starting transfers between devices, body(): lax.all_to_all(piece, 'z', 0, 0, axis_index_groups=[turned], tiled=True)  19.1 us
    ppermute x1, waiting for transfers between devices, body(): other = lax.ppermute(own, 'core', swap)  3.76 us
    all_gather x1, blocking collectives, body(): got_last = lax.all_gather(send_last, 'core', axis=0, tiled=True)  2.77 us
    ppermute x1, starting transfers between devices, body(): other = lax.ppermute(own, 'core', swap)  2.74 us
    pallas_call x1, Pallas kernels, body(): pl.pallas_call(contract, out_shape=jax.ShapeDtypeStruct((2 * aux, HALF, b...  2.6 us
  transfers between devices with their start and end apart: 2, of which 1 were waited for; matrix products, arithmetic and copies ran while one was open for 0% of the time, Pallas kernels for 0%

profile of v5, /device:TPU:1, one launch (start us, length us, event | category | flops | bytes accessed | tf_op | source)
XLA Modules:
  0.0 107.8 jit_solution(17411885180316714939)
XLA Ops:
  0.0 2.4 %prepare.1 = (bf16[16,16,128]{2,1,0:T(8,128)(2,1)}, bf16[8,64,512]{2,1,0:T(8,128)(2,1)S(1)}, bf16[7,64,512]{2,1,0:T(8,128)(2,1)S(1)}, bf16[1,64,512]{2,1,0:T(8,128)(2,1)S(1)}) custom-call(bf16[8,64,1024]{2,1,0:T(8,128)(2,1)} %tc_hbm.1, bf16[32,1024]{1,0:T(8,128)(2,1)} %den_hbm.1, s32[16,16]{1,0:T(8,128)} %pair_hbm.1, s32[16,16]{1,0:T(8,128)} %dmask_hbm.1), custom_call_target="tpu_custom_call" | custom-call | tf_op jit(solution)/shard_map/prepare/pallas_call | solution.py:179
  2.4 19.1 %all-to-all-start = ((bf16[16,16,128]{2,1,0:T(8,128)(2,1)}), bf16[16,16,128]{2,1,0:T(8,128)(2,1)S(1)}, u32[]{:S(2)}, u32[]{:S(2)}) async-start(bf16[16,16,128]{2,1,0:T(8,128)(2,1)} %get-tuple-element.12), calls=%async_computation | async-start | bytes 131072 | tf_op jit(solution)/shard_map/all_to_all | solution.py:195
  21.6 2.8 %all_gather.7.last_ref = bf16[2,64,512]{2,1,0:T(8,128)(2,1)S(1)} all-gather(bf16[1,64,512]{2,1,0:T(8,128)(2,1)S(1)} %get-tuple-element.11), channel_id=1, replica_groups=mesh['y'=4,'x'=4,'z'=16,'core'=2] {'core'}, dimensions={0}, use_global_device_ids=true | all-gather | bytes 196608 | tf_op jit(solution)/shard_map/all_gather | solution.py:197
  24.3 2.4 %all_gather.6.got_ref = bf16[14,64,512]{2,1,0:T(8,128)(2,1)S(1)} all-gather(bf16[7,64,512]{2,1,0:T(8,128)(2,1)S(1)} %get-tuple-element.10), channel_id=1, replica_groups=mesh['y'=4,'x'=4,'z'=16,'core'=2] {'core'}, dimensions={0}, use_global_device_ids=true | all-gather | bytes 1376256 | tf_op jit(solution)/shard_map/all_gather | solution.py:196
  26.8 0.1 join.1.slab_ref
  26.9 0.0 all-to-all-done.den_ref
  26.9 0.3 pack.1
  27.1 31.8 %all_to_all.20.own_ref = bf16[16,128,512]{2,1,0:T(8,128)(2,1)S(1)} all-to-all(bf16[16,128,512]{2,1,0:T(8,128)(2,1)S(1)} %pack.1), channel_id=1, replica_groups={{320,352,384,416,448,480,0,32,64,96,128,160,192,224,256,288},{321,353,3..., dimensions={0} | all-to-all | bytes 4194304 | tf_op jit(solution)/shard_map/all_to_all | solution.py:215
  59.0 2.7 %collective-permute-start = (bf16[16,128,512]{2,1,0:T(8,128)(2,1)S(1)}, bf16[16,128,512]{2,1,0:T(8,128)(2,1)S(1)}, u32[]{:S(2)}, u32[]{:S(2)}) collective-permute-start(bf16[16,128,512]{2,1,0:T(8,128)(2,1)S(1)} %all_to_all.20.own_ref), channel_id=1, source_target_pairs={{0,1},{1,0},{2,3},{3,2},{4,5},{5,4},{6,7},{7,6},{8,9},{9,8},{10,11... | collective-permute-start | bytes 6291464 | tf_op jit(solution)/shard_map/ppermute | solution.py:216
  61.7 3.8 %collective-permute-done.other_ref = bf16[16,128,512]{2,1,0:T(8,128)(2,1)S(1)} collective-permute-done((bf16[16,128,512]{2,1,0:T(8,128)(2,1)S(1)}, bf16[16,128,512]{2,1,0:T(8,128)(2,1)S(1)}, u32[]{:S(2)}, u32[]{:S(2)}) %collective-permute-start) | collective-permute-done | bytes 2097184 | tf_op jit(solution)/shard_map/ppermute | solution.py:216
  65.5 2.6 %contract.1 = bf16[16,32,1024]{2,1,0:T(8,128)(2,1)S(1)} custom-call(bf16[16,128,512]{2,1,0:T(8,128)(2,1)S(1)} %all_to_all.20.own_ref, bf16[16,128,512]{2,1,0:T(8,128)(2,1)S(1)} %collective-permute-done.other_ref), custom_call_target="tpu_custom_call" | custom-call | tf_op jit(solution)/shard_map/contract/pallas_call | solution.py:217
  68.1 19.3 %all_to_all.21.in_ref = bf16[16,32,1024]{2,1,0:T(8,128)(2,1)S(1)} all-to-all(bf16[16,32,1024]{2,1,0:T(8,128)(2,1)S(1)} %contract.1), channel_id=1, replica_groups={{320,352,384,416,448,480,0,32,64,96,128,160,192,224,256,288},{321,353,3..., dimensions={0} | all-to-all | bytes 2097152 | tf_op jit(solution)/shard_map/all_to_all | solution.py:226
  87.4 0.2 sum_aux.1
  87.6 19.4 %all_to_all.22.in_ref = f32[32,8,128]{2,1,0:T(8,128)S(1)} all-to-all(f32[32,8,128]{2,1,0:T(8,128)S(1)} %sum_aux.1), channel_id=1, replica_groups={{16,17,18,19,20,21,22,23,24,25,26,27,28,29,30,31,0,1,2,3,4,5,6,7,8,9,10..., dimensions={0} | all-to-all | bytes 262144 | tf_op jit(solution)/shard_map/all_to_all | solution.py:236
  107.0 0.8 sum_planes.1
Async XLA Ops:
  2.4 24.4 %all-to-all-start = ((bf16[16,16,128]{2,1,0:T(8,128)(2,1)}), bf16[16,16,128]{2,1,0:T(8,128)(2,1)S(1)}, u32[]{:S(2)}, u32[]{:S(2)}) async-start(bf16[16,16,128]{2,1,0:T(8,128)(2,1)} %get-tuple-element.12), calls=%async_computation | async-start | bytes 131072 | tf_op jit(solution)/shard_map/all_to_all | solution.py:195
  59.0 6.5 %collective-permute-start = (bf16[16,128,512]{2,1,0:T(8,128)(2,1)S(1)}, bf16[16,128,512]{2,1,0:T(8,128)(2,1)S(1)}, u32[]{:S(2)}, u32[]{:S(2)}) collective-permute-start(bf16[16,128,512]{2,1,0:T(8,128)(2,1)S(1)} %all_to_all.20.own_ref), channel_id=1, source_target_pairs={{0,1},{1,0},{2,3},{3,2},{4,5},{5,4},{6,7},{7,6},{8,9},{9,8},{10,11... | collective-permute-start | bytes 6291464 | tf_op jit(solution)/shard_map/ppermute | solution.py:216

commit v6 on v5

--- a/solution.py
+++ b/solution.py
@@ -146,25 +146,29 @@
 
 def sum_aux(in_ref, out_ref):
     basis = in_ref.shape[2]
-    for tile in range(basis // LANES):
+    half = basis // LANES // 2
+
+    def total(tile):
         cols = slice(tile * LANES, (tile + 1) * LANES)
-        total = in_ref[0, :, cols].astype(jnp.float32)
+        value = in_ref[0, :, cols].astype(jnp.float32)
         for k in range(1, in_ref.shape[0]):
-            total = total + in_ref[k, :, cols].astype(jnp.float32)
-        groups = [total[8 * g : 8 * g + 8] for g in range(4)]
+            value = value + in_ref[k, :, cols].astype(jnp.float32)
+        return [value[8 * g : 8 * g + 8] for g in range(4)]
+
+    for tile in range(half):
+        cores = [total(tile), total(tile + half)]
         for q in range(4):
-            dest = ((tile % 4 * 4 + q + TURN) % PLANES) * 2 + tile // 4
-            out_ref[dest] = gather_groups(groups, q * HALF)
+            slot = (tile * 4 + q + TURN) % PLANES
+            both = jnp.concatenate([gather_groups(groups, q * HALF) for groups in cores])
+            out_ref[slot * PACK : (slot + 1) * PACK, :] = both.astype(out_ref.dtype)
 
 
 def sum_planes(in_ref, out_ref):
-    totals = []
-    for core in range(2):
-        total = in_ref[core]
-        for z in range(1, in_ref.shape[0] // 2):
-            total = total + in_ref[2 * z + core]
-        totals += [total[:, g * HALF : (g + 1) * HALF] for g in range(4)]
-    out_ref[...] = jnp.concatenate(totals, axis=0).T
+    total = in_ref[:PACK, :].astype(jnp.float32)
+    for z in range(1, PLANES):
+        total = total + in_ref[z * PACK : (z + 1) * PACK, :].astype(jnp.float32)
+    parts = [total[8 * core : 8 * core + 8, g * HALF : (g + 1) * HALF] for core in range(2) for g in range(4)]
+    out_ref[...] = jnp.concatenate(parts, axis=0).T
 
 
 def body(three_centre, density, pair_mask, density_mask):
@@ -226,7 +230,7 @@
     pieces = lax.all_to_all(partial, ROW, 0, 0, axis_index_groups=from_corner, tiled=True)
     packed = pl.pallas_call(
         sum_aux,
-        out_shape=jax.ShapeDtypeStruct((32, 8, LANES), f32),
+        out_shape=jax.ShapeDtypeStruct((PLANES * PACK, LANES), bf16),
         in_specs=[vmem()],
         out_specs=vmem(),
         compiler_params=pltpu.CompilerParams(vmem_limit_bytes=16 << 20),

time: 108 us -> 106 us (0.981)
  blocking collectives: 75.7 us -> 73.1 us
    all_to_all x1, blocking collectives: 19.4 us -> 16.8 us  [body(): lax.all_to_all(packed, COL, 0, 0, axis_index_groups=pairs, tiled=True)]
where the time goes in v6:
time: 106 us; the launch traced here: 105 us
  blocking collectives  73.1 us (69%)
  starting transfers between devices  21.9 us (21%)
  Pallas kernels  6.33 us (6%)
  waiting for transfers between devices  3.77 us (4%)
    all_to_all x1, blocking collectives, body(): lax.all_to_all(slabs, ROW, 0, 0, axis_index_groups=from_corner, tiled=True)  31.8 us
    all_to_all x1, blocking collectives, body(): lax.all_to_all(partial, ROW, 0, 0, axis_index_groups=from_corner, tiled=T...  19.3 us
    all_to_all x1, starting transfers between devices, body(): lax.all_to_all(piece, 'z', 0, 0, axis_index_groups=[turned], tiled=True)  19.1 us
    all_to_all x1, blocking collectives, body(): lax.all_to_all(packed, COL, 0, 0, axis_index_groups=pairs, tiled=True)  16.8 us
    ppermute x1, waiting for transfers between devices, body(): other = lax.ppermute(own, 'core', swap)  3.76 us
    all_gather x1, blocking collectives, body(): got_last = lax.all_gather(send_last, 'core', axis=0, tiled=True)  2.77 us
    ppermute x1, starting transfers between devices, body(): other = lax.ppermute(own, 'core', swap)  2.74 us
    pallas_call x1, Pallas kernels, body(): pl.pallas_call(contract, out_shape=jax.ShapeDtypeStruct((2 * aux, HALF, b...  2.6 us
  transfers between devices with their start and end apart: 2, of which 1 were waited for; matrix products, arithmetic and copies ran while one was open for 0% of the time, Pallas kernels for 0%

profile of v6, /device:TPU:1, one launch (start us, length us, event | category | flops | bytes accessed | tf_op | source)
XLA Modules:
  0.0 105.2 jit_solution(8989722186653199283)
XLA Ops:
  0.0 2.4 %prepare.1 = (bf16[16,16,128]{2,1,0:T(8,128)(2,1)}, bf16[8,64,512]{2,1,0:T(8,128)(2,1)S(1)}, bf16[7,64,512]{2,1,0:T(8,128)(2,1)S(1)}, bf16[1,64,512]{2,1,0:T(8,128)(2,1)S(1)}) custom-call(bf16[8,64,1024]{2,1,0:T(8,128)(2,1)} %tc_hbm.1, bf16[32,1024]{1,0:T(8,128)(2,1)} %den_hbm.1, s32[16,16]{1,0:T(8,128)} %pair_hbm.1, s32[16,16]{1,0:T(8,128)} %dmask_hbm.1), custom_call_target="tpu_custom_call" | custom-call | tf_op jit(solution)/shard_map/prepare/pallas_call | solution.py:183
  2.4 19.1 %all-to-all-start = ((bf16[16,16,128]{2,1,0:T(8,128)(2,1)}), bf16[16,16,128]{2,1,0:T(8,128)(2,1)S(1)}, u32[]{:S(2)}, u32[]{:S(2)}) async-start(bf16[16,16,128]{2,1,0:T(8,128)(2,1)} %get-tuple-element.12), calls=%async_computation | async-start | bytes 131072 | tf_op jit(solution)/shard_map/all_to_all | solution.py:199
  21.6 2.8 %all_gather.7.last_ref = bf16[2,64,512]{2,1,0:T(8,128)(2,1)S(1)} all-gather(bf16[1,64,512]{2,1,0:T(8,128)(2,1)S(1)} %get-tuple-element.11), channel_id=1, replica_groups=mesh['y'=4,'x'=4,'z'=16,'core'=2] {'core'}, dimensions={0}, use_global_device_ids=true | all-gather | bytes 196608 | tf_op jit(solution)/shard_map/all_gather | solution.py:201
  24.3 2.4 %all_gather.6.got_ref = bf16[14,64,512]{2,1,0:T(8,128)(2,1)S(1)} all-gather(bf16[7,64,512]{2,1,0:T(8,128)(2,1)S(1)} %get-tuple-element.10), channel_id=1, replica_groups=mesh['y'=4,'x'=4,'z'=16,'core'=2] {'core'}, dimensions={0}, use_global_device_ids=true | all-gather | bytes 1376256 | tf_op jit(solution)/shard_map/all_gather | solution.py:200
  26.8 0.1 join.1.slab_ref
  26.9 0.0 all-to-all-done.den_ref
  26.9 0.3 pack.1
  27.1 31.8 %all_to_all.26.own_ref = bf16[16,128,512]{2,1,0:T(8,128)(2,1)S(1)} all-to-all(bf16[16,128,512]{2,1,0:T(8,128)(2,1)S(1)} %pack.1), channel_id=1, replica_groups={{320,352,384,416,448,480,0,32,64,96,128,160,192,224,256,288},{321,353,3..., dimensions={0} | all-to-all | bytes 4194304 | tf_op jit(solution)/shard_map/all_to_all | solution.py:219
  59.0 2.7 %collective-permute-start = (bf16[16,128,512]{2,1,0:T(8,128)(2,1)S(1)}, bf16[16,128,512]{2,1,0:T(8,128)(2,1)S(1)}, u32[]{:S(2)}, u32[]{:S(2)}) collective-permute-start(bf16[16,128,512]{2,1,0:T(8,128)(2,1)S(1)} %all_to_all.26.own_ref), channel_id=1, source_target_pairs={{0,1},{1,0},{2,3},{3,2},{4,5},{5,4},{6,7},{7,6},{8,9},{9,8},{10,11... | collective-permute-start | bytes 6291464 | tf_op jit(solution)/shard_map/ppermute | solution.py:220
  61.7 3.8 %collective-permute-done.other_ref = bf16[16,128,512]{2,1,0:T(8,128)(2,1)S(1)} collective-permute-done((bf16[16,128,512]{2,1,0:T(8,128)(2,1)S(1)}, bf16[16,128,512]{2,1,0:T(8,128)(2,1)S(1)}, u32[]{:S(2)}, u32[]{:S(2)}) %collective-permute-start) | collective-permute-done | bytes 2097184 | tf_op jit(solution)/shard_map/ppermute | solution.py:220
  65.5 2.6 %contract.1 = bf16[16,32,1024]{2,1,0:T(8,128)(2,1)S(1)} custom-call(bf16[16,128,512]{2,1,0:T(8,128)(2,1)S(1)} %all_to_all.26.own_ref, bf16[16,128,512]{2,1,0:T(8,128)(2,1)S(1)} %collective-permute-done.other_ref), custom_call_target="tpu_custom_call" | custom-call | tf_op jit(solution)/shard_map/contract/pallas_call | solution.py:221
  68.1 19.3 %all_to_all.27.in_ref = bf16[16,32,1024]{2,1,0:T(8,128)(2,1)S(1)} all-to-all(bf16[16,32,1024]{2,1,0:T(8,128)(2,1)S(1)} %contract.1), channel_id=1, replica_groups={{320,352,384,416,448,480,0,32,64,96,128,160,192,224,256,288},{321,353,3..., dimensions={0} | all-to-all | bytes 2097152 | tf_op jit(solution)/shard_map/all_to_all | solution.py:230
  87.4 0.2 sum_aux.1
  87.6 16.8 %all_to_all.28 = bf16[32,8,128]{2,1,0:T(8,128)(2,1)S(1)} all-to-all(bf16[32,8,128]{2,1,0:T(8,128)(2,1)S(1)} %bitcast.3), channel_id=1, replica_groups={{16,17,18,19,20,21,22,23,24,25,26,27,28,29,30,31,0,1,2,3,4,5,6,7,8,9,10..., dimensions={0} | all-to-all | bytes 131072 | tf_op jit(solution)/shard_map/all_to_all | solution.py:240
  104.4 0.8 sum_planes.1
Async XLA Ops:
  2.4 24.4 %all-to-all-start = ((bf16[16,16,128]{2,1,0:T(8,128)(2,1)}), bf16[16,16,128]{2,1,0:T(8,128)(2,1)S(1)}, u32[]{:S(2)}, u32[]{:S(2)}) async-start(bf16[16,16,128]{2,1,0:T(8,128)(2,1)} %get-tuple-element.12), calls=%async_computation | async-start | bytes 131072 | tf_op jit(solution)/shard_map/all_to_all | solution.py:199
  59.0 6.5 %collective-permute-start = (bf16[16,128,512]{2,1,0:T(8,128)(2,1)S(1)}, bf16[16,128,512]{2,1,0:T(8,128)(2,1)S(1)}, u32[]{:S(2)}, u32[]{:S(2)}) collective-permute-start(bf16[16,128,512]{2,1,0:T(8,128)(2,1)S(1)} %all_to_all.26.own_ref), channel_id=1, source_target_pairs={{0,1},{1,0},{2,3},{3,2},{4,5},{5,4},{6,7},{7,6},{8,9},{9,8},{10,11... | collective-permute-start | bytes 6291464 | tf_op jit(solution)/shard_map/ppermute | solution.py:220

commit v7 on v6

--- a/solution.py
+++ b/solution.py
@@ -16,6 +16,7 @@
 LANES = 128
 PACK = 16
 PLANES = 16
+FIRST = 11
 TURN = PLANES // 2
 ROWS = 16
 SHIFT = 10
@@ -30,7 +31,7 @@
 
 
 def prepare(
-    tc_hbm, den_hbm, pair_hbm, dmask_hbm, piece_ref, keep_ref, send_ref, last_ref, tc, den, pair, dmask, sems
+    tc_hbm, den_hbm, pair_hbm, dmask_hbm, piece_hbm, keep_ref, send_ref, last_ref, tc, den, pieces, pair, dmask, sems
 ):
     row = lax.axis_index("y") * 4 + lax.axis_index("x")
     core = lax.axis_index("core")
@@ -60,7 +61,9 @@
     a = dmask[mask_row, 2 * tile].astype(jnp.float32)
     b = dmask[mask_row, 2 * tile + 1].astype(jnp.float32)
     scaled = (den[...].astype(jnp.float32) * jnp.where(low, a, b)).astype(jnp.bfloat16)
-    piece_ref[...] = jnp.broadcast_to(scaled[None], piece_ref.shape)
+    pieces[...] = jnp.broadcast_to(scaled[None], pieces.shape)
+    hand_over = pltpu.make_async_copy(pieces, piece_hbm, sems.at[3 + aux])
+    hand_over.start()
     picks = []
     for t in range(basis // wide):
         s = [pair[4 * t + b, row].astype(jnp.float32) for b in range(4)]
@@ -81,6 +84,7 @@
             send_ref[k : k + inside, :, cols] = out[:inside, :, LANES:]
             if inside < step:
                 last_ref[:, :, cols] = out[inside:, :, LANES:]
+    hand_over.wait()
 
 
 def join(keep_ref, got_ref, last_ref, out_ref):
@@ -96,10 +100,9 @@
     parts, height, width = slab_ref.shape
     out_ref[:, :height, :] = slab_ref[...]
     groups = width // LANES
-    each = den_ref.shape[0] // groups
+    each = PLANES // groups
     for g in range(groups):
-        slot = (each * g + TURN) % PLANES
-        part = den_ref[slot : slot + each].reshape(each * PACK, LANES)
+        part = jnp.concatenate([den_ref[(z - FIRST) % PLANES] for z in range(each * g, each * (g + 1))])
         spread = jnp.broadcast_to(part[None], (parts, each * PACK, LANES))
         out_ref[:, height:, g * LANES : (g + 1) * LANES] = spread
 
@@ -184,19 +187,20 @@
         prepare,
         out_shape=(jax.ShapeDtypeStruct((planes, PACK, LANES), bf16), half, most, last),
         in_specs=[pl.BlockSpec(memory_space=pltpu.HBM)] * 4,
-        out_specs=(vmem(),) * 4,
+        out_specs=(pl.BlockSpec(memory_space=pltpu.HBM), vmem(), vmem(), vmem()),
         scratch_shapes=[
             VMEM(three_centre.shape, bf16),
             VMEM((PACK, LANES), bf16),
+            VMEM((planes, PACK, LANES), bf16),
             SMEM(pair_mask.shape, jnp.int32),
             SMEM(density_mask.shape, jnp.int32),
-            pltpu.SemaphoreType.DMA((3 + aux,)),
+            pltpu.SemaphoreType.DMA((4 + aux,)),
         ],
         compiler_params=pltpu.CompilerParams(vmem_limit_bytes=40 << 20),
         name="prepare",
     )(*(pltpu.with_memory_space_constraint(a, pltpu.HBM) for a in (three_centre, density, pair_mask, density_mask)))
-    turned = [(i + TURN) % PLANES for i in range(PLANES)]
-    along_z = lax.all_to_all(piece, "z", 0, 0, axis_index_groups=[turned], tiled=True)
+    late_first = [(i + FIRST) % PLANES for i in range(PLANES)]
+    along_z = lax.all_to_all(piece, "z", 0, 0, axis_index_groups=[late_first], tiled=True)
     got = lax.all_gather(send, "core", axis=0, tiled=True)
     got_last = lax.all_gather(send_last, "core", axis=0, tiled=True)
     both = pl.pallas_call(
@@ -236,6 +240,7 @@
         compiler_params=pltpu.CompilerParams(vmem_limit_bytes=16 << 20),
         name="sum_aux",
     )(pieces)
+    turned = [(i + TURN) % PLANES for i in range(PLANES)]
     pairs = [[2 * z + c for z in turned for c in range(2)]]
     arrived = lax.all_to_all(packed, COL, 0, 0, axis_index_groups=pairs, tiled=True)
     return pl.pallas_call(

time: 106 us -> 104 us (0.981)
  starting transfers between devices: 21.9 us -> 19.8 us
    all_to_all x1, starting transfers between devices: 19.1 us -> 16.4 us  [body(): lax.all_to_all(piece, 'z', 0, 0, axis_index_groups=[late_first], tiled=True)]
  transfers between devices with their start and end apart: 2 -> 2, of which waited for: 1 -> 2; matrix products, arithmetic and copies ran while one was open for 0% -> 0% of each run, Pallas kernels for 0% -> 0%
where the time goes in v7:
time: 104 us; the launch traced here: 103 us
  blocking collectives  73.2 us (70%)
  starting transfers between devices  19.8 us (19%)
  Pallas kernels  5.96 us (6%)
  waiting for transfers between devices  4.21 us (4%)
    all_to_all x1, blocking collectives, body(): lax.all_to_all(slabs, ROW, 0, 0, axis_index_groups=from_corner, tiled=True)  31.6 us
    all_to_all x1, blocking collectives, body(): lax.all_to_all(partial, ROW, 0, 0, axis_index_groups=from_corner, tiled=T...  19.5 us
    all_to_all x1, blocking collectives, body(): lax.all_to_all(packed, COL, 0, 0, axis_index_groups=pairs, tiled=True)  16.9 us
    all_to_all x1, starting transfers between devices, body(): lax.all_to_all(piece, 'z', 0, 0, axis_index_groups=[late_first], tiled=True)  16.4 us
    ppermute x1, waiting for transfers between devices, body(): other = lax.ppermute(own, 'core', swap)  3.76 us
    ppermute x1, starting transfers between devices, body(): other = lax.ppermute(own, 'core', swap)  3.33 us
    all_gather x1, blocking collectives, body(): got_last = lax.all_gather(send_last, 'core', axis=0, tiled=True)  2.77 us
    pallas_call x1, Pallas kernels, body(): pl.pallas_call(contract, out_shape=jax.ShapeDtypeStruct((2 * aux, HALF, b...  2.6 us
  transfers between devices with their start and end apart: 2, of which 2 were waited for; matrix products, arithmetic and copies ran while one was open for 0% of the time, Pallas kernels for 0%

profile of v7, /device:TPU:1, one launch (start us, length us, event | category | flops | bytes accessed | tf_op | source)
XLA Modules:
  0.0 103.2 jit_solution(15023065923688668024)
XLA Ops:
  0.0 2.0 %prepare.1 = (bf16[16,16,128]{2,1,0:T(8,128)(2,1)}, bf16[8,64,512]{2,1,0:T(8,128)(2,1)S(1)}, bf16[7,64,512]{2,1,0:T(8,128)(2,1)S(1)}, bf16[1,64,512]{2,1,0:T(8,128)(2,1)S(1)}) custom-call(bf16[8,64,1024]{2,1,0:T(8,128)(2,1)} %tc_hbm.1, bf16[32,1024]{1,0:T(8,128)(2,1)} %den_hbm.1, s32[16,16]{1,0:T(8,128)} %pair_hbm.1, s32[16,16]{1,0:T(8,128)} %dmask_hbm.1), custom_call_target="tpu_custom_call" | custom-call | tf_op jit(solution)/shard_map/prepare/pallas_call | solution.py:186
  2.0 16.4 %all-to-all-start = ((bf16[16,16,128]{2,1,0:T(8,128)(2,1)}), bf16[16,16,128]{2,1,0:T(8,128)(2,1)S(1)}, u32[]{:S(2)}, u32[]{:S(2)}) async-start(bf16[16,16,128]{2,1,0:T(8,128)(2,1)} %get-tuple-element.12), calls=%async_computation | async-start | bytes 131072 | tf_op jit(solution)/shard_map/all_to_all | solution.py:203
  18.5 2.8 %all_gather.7.last_ref = bf16[2,64,512]{2,1,0:T(8,128)(2,1)S(1)} all-gather(bf16[1,64,512]{2,1,0:T(8,128)(2,1)S(1)} %get-tuple-element.11), channel_id=1, replica_groups=mesh['y'=4,'x'=4,'z'=16,'core'=2] {'core'}, dimensions={0}, use_global_device_ids=true | all-gather | bytes 196608 | tf_op jit(solution)/shard_map/all_gather | solution.py:205
  21.3 2.4 %all_gather.6.got_ref = bf16[14,64,512]{2,1,0:T(8,128)(2,1)S(1)} all-gather(bf16[7,64,512]{2,1,0:T(8,128)(2,1)S(1)} %get-tuple-element.10), channel_id=1, replica_groups=mesh['y'=4,'x'=4,'z'=16,'core'=2] {'core'}, dimensions={0}, use_global_device_ids=true | all-gather | bytes 1376256 | tf_op jit(solution)/shard_map/all_gather | solution.py:204
  23.7 0.1 join.1.slab_ref
  23.8 0.4 all-to-all-done.den_ref
  24.2 0.3 pack.1
  24.5 31.6 %all_to_all.26.own_ref = bf16[16,128,512]{2,1,0:T(8,128)(2,1)S(1)} all-to-all(bf16[16,128,512]{2,1,0:T(8,128)(2,1)S(1)} %pack.1), channel_id=1, replica_groups={{320,352,384,416,448,480,0,32,64,96,128,160,192,224,256,288},{321,353,3..., dimensions={0} | all-to-all | bytes 4194304 | tf_op jit(solution)/shard_map/all_to_all | solution.py:223
  56.1 3.3 %collective-permute-start = (bf16[16,128,512]{2,1,0:T(8,128)(2,1)S(1)}, bf16[16,128,512]{2,1,0:T(8,128)(2,1)S(1)}, u32[]{:S(2)}, u32[]{:S(2)}) collective-permute-start(bf16[16,128,512]{2,1,0:T(8,128)(2,1)S(1)} %all_to_all.26.own_ref), channel_id=1, source_target_pairs={{0,1},{1,0},{2,3},{3,2},{4,5},{5,4},{6,7},{7,6},{8,9},{9,8},{10,11... | collective-permute-start | bytes 6291464 | tf_op jit(solution)/shard_map/ppermute | solution.py:224
  59.5 3.8 %collective-permute-done.other_ref = bf16[16,128,512]{2,1,0:T(8,128)(2,1)S(1)} collective-permute-done((bf16[16,128,512]{2,1,0:T(8,128)(2,1)S(1)}, bf16[16,128,512]{2,1,0:T(8,128)(2,1)S(1)}, u32[]{:S(2)}, u32[]{:S(2)}) %collective-permute-start) | collective-permute-done | bytes 2097184 | tf_op jit(solution)/shard_map/ppermute | solution.py:224
  63.2 2.6 %contract.1 = bf16[16,32,1024]{2,1,0:T(8,128)(2,1)S(1)} custom-call(bf16[16,128,512]{2,1,0:T(8,128)(2,1)S(1)} %all_to_all.26.own_ref, bf16[16,128,512]{2,1,0:T(8,128)(2,1)S(1)} %collective-permute-done.other_ref), custom_call_target="tpu_custom_call" | custom-call | tf_op jit(solution)/shard_map/contract/pallas_call | solution.py:225
  65.8 19.5 %all_to_all.27.in_ref = bf16[16,32,1024]{2,1,0:T(8,128)(2,1)S(1)} all-to-all(bf16[16,32,1024]{2,1,0:T(8,128)(2,1)S(1)} %contract.1), channel_id=1, replica_groups={{320,352,384,416,448,480,0,32,64,96,128,160,192,224,256,288},{321,353,3..., dimensions={0} | all-to-all | bytes 2097152 | tf_op jit(solution)/shard_map/all_to_all | solution.py:234
  85.3 0.2 sum_aux.1
  85.5 16.9 %all_to_all.28 = bf16[32,8,128]{2,1,0:T(8,128)(2,1)S(1)} all-to-all(bf16[32,8,128]{2,1,0:T(8,128)(2,1)S(1)} %bitcast.3), channel_id=1, replica_groups={{16,17,18,19,20,21,22,23,24,25,26,27,28,29,30,31,0,1,2,3,4,5,6,7,8,9,10..., dimensions={0} | all-to-all | bytes 131072 | tf_op jit(solution)/shard_map/all_to_all | solution.py:245
  102.4 0.8 sum_planes.1
Async XLA Ops:
  2.0 22.2 %all-to-all-start = ((bf16[16,16,128]{2,1,0:T(8,128)(2,1)}), bf16[16,16,128]{2,1,0:T(8,128)(2,1)S(1)}, u32[]{:S(2)}, u32[]{:S(2)}) async-start(bf16[16,16,128]{2,1,0:T(8,128)(2,1)} %get-tuple-element.12), calls=%async_computation | async-start | bytes 131072 | tf_op jit(solution)/shard_map/all_to_all | solution.py:203
  56.1 7.1 %collective-permute-start = (bf16[16,128,512]{2,1,0:T(8,128)(2,1)S(1)}, bf16[16,128,512]{2,1,0:T(8,128)(2,1)S(1)}, u32[]{:S(2)}, u32[]{:S(2)}) collective-permute-start(bf16[16,128,512]{2,1,0:T(8,128)(2,1)S(1)} %all_to_all.26.own_ref), channel_id=1, source_target_pairs={{0,1},{1,0},{2,3},{3,2},{4,5},{5,4},{6,7},{7,6},{8,9},{9,8},{10,11... | collective-permute-start | bytes 6291464 | tf_op jit(solution)/shard_map/ppermute | solution.py:224

commit v8 on v7

--- a/solution.py
+++ b/solution.py
@@ -107,38 +107,50 @@
         out_ref[:, height:, g * LANES : (g + 1) * LANES] = spread
 
 
-def contract(own_ref, other_ref, out_ref, den):
+def place(ref, den):
+    height = ref.shape[1] // 2
+    tiles = den.shape[-1] // LANES
+    groups = ref.shape[2] // LANES
+    each = PLANES // groups
+    for k in range(ROWS):
+        row = (k + SHIFT) % ROWS
+        cols = slice(row % tiles * LANES, (row % tiles + 1) * LANES)
+        for g in range(groups):
+            part = ref[k, height:, g * LANES : (g + 1) * LANES].reshape(each, PACK, LANES)
+            den[each * g : each * (g + 1), row // tiles, :, cols] = part
+
+
+def slab_rows(ref, start, count):
+    rows = pl.ds(start, count)
+    turned = jnp.concatenate([ref[ROWS - SHIFT :, rows, :], ref[: ROWS - SHIFT, rows, :]])
+    return turned.reshape(ROWS * count, ref.shape[2])
+
+
+def half_sum(ref, own_ref, side, den):
+    place(ref, den)
+    own = slab_rows(own_ref, pl.multiple_of(side * HALF, HALF), HALF)
+    density = den[...].reshape(ROWS * HALF, den.shape[-1])
+    return lax.dot_general(own, density, (((0,), (0,)), ((), ())), preferred_element_type=jnp.float32)
+
+
+def begin(own_ref, sum_ref, den):
+    sum_ref[...] = half_sum(own_ref, own_ref, lax.axis_index("core"), den)
+
+
+def contract(own_ref, other_ref, sum_ref, out_ref, den):
     core = lax.axis_index("core")
-    parts, both, width = own_ref.shape
-    height = both // 2
-    tiles = den.shape[-1] // LANES
-    groups = width // LANES
-    each = den.shape[0] // groups
-    for ref, side in ((own_ref, core), (other_ref, 1 - core)):
-        for k in range(ROWS):
-            row = (k + SHIFT) % ROWS
-            cols = slice(row % tiles * LANES, (row % tiles + 1) * LANES)
-            for g in range(groups):
-                part = ref[k, height:, g * LANES : (g + 1) * LANES].reshape(each, PACK, LANES)
-                den[each * g : each * (g + 1), side, row // tiles, :, cols] = part
-
-    def slab(ref):
-        turned = jnp.concatenate([ref[ROWS - SHIFT :, :height, :], ref[: ROWS - SHIFT, :height, :]])
-        return turned.reshape(parts * height, width)
+    width = own_ref.shape[2]
 
     def put(value, cols):
         value = value.astype(jnp.bfloat16).reshape(ROWS, out_ref.shape[1], width)
         out_ref[: ROWS - SHIFT, :, cols] = value[SHIFT:]
         out_ref[ROWS - SHIFT :, :, cols] = value[:SHIFT]
 
-    own = slab(own_ref)
-    density = den[...].reshape(parts * height, den.shape[-1])
-    built = lax.dot_general(
-        own, density, (((0,), (0,)), ((), ())), preferred_element_type=jnp.float32
-    ).astype(jnp.bfloat16)
+    built = (sum_ref[...] + half_sum(other_ref, own_ref, 1 - core, den)).astype(jnp.bfloat16)
+    own = slab_rows(own_ref, 0, BLK)
     put(jnp.dot(built, own, preferred_element_type=jnp.float32), pl.ds(pl.multiple_of(core * width, LANES), width))
     put(
-        jnp.dot(built, slab(other_ref), preferred_element_type=jnp.float32),
+        jnp.dot(built, slab_rows(other_ref, 0, BLK), preferred_element_type=jnp.float32),
         pl.ds(pl.multiple_of((1 - core) * width, LANES), width),
     )
 
@@ -222,15 +234,26 @@
     from_corner = [[(i + SHIFT) % ROWS for i in range(ROWS)]]
     own = lax.all_to_all(slabs, ROW, 0, 0, axis_index_groups=from_corner, tiled=True)
     other = lax.ppermute(own, "core", swap)
+    den_scratch = VMEM((planes, 2, PACK, basis), bf16)
+    own_sum = pl.pallas_call(
+        begin,
+        out_shape=jax.ShapeDtypeStruct((width, basis), f32),
+        in_specs=[vmem()],
+        out_specs=vmem(),
+        scratch_shapes=[den_scratch],
+        compiler_params=pltpu.CompilerParams(vmem_limit_bytes=32 << 20),
+        cost_estimate=pl.CostEstimate(flops=width * width * basis * 2, bytes_accessed=4 << 20, transcendentals=0),
+        name="begin",
+    )(own)
     partial = pl.pallas_call(
         contract,
         out_shape=jax.ShapeDtypeStruct((2 * aux, HALF, basis), bf16),
-        in_specs=[vmem()] * 2,
-        out_specs=vmem(),
-        scratch_shapes=[VMEM((planes, 2, 2, PACK, basis), bf16)],
+        in_specs=[vmem()] * 3,
+        out_specs=vmem(),
+        scratch_shapes=[den_scratch],
         compiler_params=pltpu.CompilerParams(vmem_limit_bytes=40 << 20),
         name="contract",
-    )(own, other)
+    )(own, other, own_sum)
     pieces = lax.all_to_all(partial, ROW, 0, 0, axis_index_groups=from_corner, tiled=True)
     packed = pl.pallas_call(
         sum_aux,

time: 104 us -> 103 us (level)
  transfers between devices with their start and end apart: 2 -> 2, of which waited for: 2 -> 2; matrix products, arithmetic and copies ran while one was open for 0% -> 0% of each run, Pallas kernels for 0% -> 1%
where the time goes in v8:
time: 103 us
  blocking collectives  73.2 us (71%)
  starting transfers between devices  19.8 us (19%)
  Pallas kernels  6.11 us (6%)
  waiting for transfers between devices  3.39 us (3%)
    all_to_all x1, blocking collectives, body(): lax.all_to_all(slabs, ROW, 0, 0, axis_index_groups=from_corner, tiled=True)  31.6 us
    all_to_all x1, blocking collectives, body(): lax.all_to_all(partial, ROW, 0, 0, axis_index_groups=from_corner, tiled=T...  19.5 us
    all_to_all x1, blocking collectives, body(): lax.all_to_all(packed, COL, 0, 0, axis_index_groups=pairs, tiled=True)  16.9 us
    all_to_all x1, starting transfers between devices, body(): lax.all_to_all(piece, 'z', 0, 0, axis_index_groups=[late_first], tiled=True)  16.4 us
    ppermute x1, starting transfers between devices, body(): other = lax.ppermute(own, 'core', swap)  3.33 us
    ppermute x1, waiting for transfers between devices, body(): other = lax.ppermute(own, 'core', swap)  2.94 us
    all_gather x1, blocking collectives, body(): got_last = lax.all_gather(send_last, 'core', axis=0, tiled=True)  2.77 us
    all_gather x1, blocking collectives, body(): got = lax.all_gather(send, 'core', axis=0, tiled=True)  2.45 us
  transfers between devices with their start and end apart: 2, of which 2 were waited for; matrix products, arithmetic and copies ran while one was open for 0% of the time, Pallas kernels for 1%

profile of v8, /device:TPU:1, one launch (start us, length us, event | category | flops | bytes accessed | tf_op | source)
XLA Modules:
  0.0 102.5 jit_solution(7610824046750634316)
XLA Ops:
  0.0 2.0 %prepare.1 = (bf16[16,16,128]{2,1,0:T(8,128)(2,1)}, bf16[8,64,512]{2,1,0:T(8,128)(2,1)S(1)}, bf16[7,64,512]{2,1,0:T(8,128)(2,1)S(1)}, bf16[1,64,512]{2,1,0:T(8,128)(2,1)S(1)}) custom-call(bf16[8,64,1024]{2,1,0:T(8,128)(2,1)} %tc_hbm.1, bf16[32,1024]{1,0:T(8,128)(2,1)} %den_hbm.1, s32[16,16]{1,0:T(8,128)} %pair_hbm.1, s32[16,16]{1,0:T(8,128)} %dmask_hbm.1), custom_call_target="tpu_custom_call" | custom-call | tf_op jit(solution)/shard_map/prepare/pallas_call | solution.py:198
  2.0 16.4 %all-to-all-start = ((bf16[16,16,128]{2,1,0:T(8,128)(2,1)}), bf16[16,16,128]{2,1,0:T(8,128)(2,1)S(1)}, u32[]{:S(2)}, u32[]{:S(2)}) async-start(bf16[16,16,128]{2,1,0:T(8,128)(2,1)} %get-tuple-element.12), calls=%async_computation | async-start | bytes 131072 | tf_op jit(solution)/shard_map/all_to_all | solution.py:215
  18.5 2.8 %all_gather.7.last_ref = bf16[2,64,512]{2,1,0:T(8,128)(2,1)S(1)} all-gather(bf16[1,64,512]{2,1,0:T(8,128)(2,1)S(1)} %get-tuple-element.11), channel_id=1, replica_groups=mesh['y'=4,'x'=4,'z'=16,'core'=2] {'core'}, dimensions={0}, use_global_device_ids=true | all-gather | bytes 196608 | tf_op jit(solution)/shard_map/all_gather | solution.py:217
  21.3 2.4 %all_gather.6.got_ref = bf16[14,64,512]{2,1,0:T(8,128)(2,1)S(1)} all-gather(bf16[7,64,512]{2,1,0:T(8,128)(2,1)S(1)} %get-tuple-element.10), channel_id=1, replica_groups=mesh['y'=4,'x'=4,'z'=16,'core'=2] {'core'}, dimensions={0}, use_global_device_ids=true | all-gather | bytes 1376256 | tf_op jit(solution)/shard_map/all_gather | solution.py:216
  23.7 0.1 join.1.slab_ref
  23.8 0.4 all-to-all-done.den_ref
  24.2 0.3 pack.1
  24.5 31.6 %all_to_all.26.own_ref = bf16[16,128,512]{2,1,0:T(8,128)(2,1)S(1)} all-to-all(bf16[16,128,512]{2,1,0:T(8,128)(2,1)S(1)} %pack.1), channel_id=1, replica_groups={{320,352,384,416,448,480,0,32,64,96,128,160,192,224,256,288},{321,353,3..., dimensions={0} | all-to-all | bytes 4194304 | tf_op jit(solution)/shard_map/all_to_all | solution.py:235
  56.1 3.3 %collective-permute-start = (bf16[16,128,512]{2,1,0:T(8,128)(2,1)S(1)}, bf16[16,128,512]{2,1,0:T(8,128)(2,1)S(1)}, u32[]{:S(2)}, u32[]{:S(2)}) collective-permute-start(bf16[16,128,512]{2,1,0:T(8,128)(2,1)S(1)} %all_to_all.26.own_ref), channel_id=1, source_target_pairs={{0,1},{1,0},{2,3},{3,2},{4,5},{5,4},{6,7},{7,6},{8,9},{9,8},{10,11... | collective-permute-start | bytes 6291464 | tf_op jit(solution)/shard_map/ppermute | solution.py:236
  59.5 0.8 begin.1.sum_ref
  60.3 2.9 %collective-permute-done.other_ref = bf16[16,128,512]{2,1,0:T(8,128)(2,1)S(1)} collective-permute-done((bf16[16,128,512]{2,1,0:T(8,128)(2,1)S(1)}, bf16[16,128,512]{2,1,0:T(8,128)(2,1)S(1)}, u32[]{:S(2)}, u32[]{:S(2)}) %collective-permute-start) | collective-permute-done | bytes 2097184 | tf_op jit(solution)/shard_map/ppermute | solution.py:236
  63.2 1.9 %contract.1 = bf16[16,32,1024]{2,1,0:T(8,128)(2,1)S(1)} custom-call(bf16[16,128,512]{2,1,0:T(8,128)(2,1)S(1)} %all_to_all.26.own_ref, bf16[16,128,512]{2,1,0:T(8,128)(2,1)S(1)} %collective-permute-done.other_ref, f32[512,1024]{1,0:T(8,128)S(1)} %begin.1.sum_ref), custom_call_target="tpu_custom_call" | custom-call | tf_op jit(solution)/shard_map/contract/pallas_call | solution.py:248
  65.2 19.5 %all_to_all.27.in_ref = bf16[16,32,1024]{2,1,0:T(8,128)(2,1)S(1)} all-to-all(bf16[16,32,1024]{2,1,0:T(8,128)(2,1)S(1)} %contract.1), channel_id=1, replica_groups={{320,352,384,416,448,480,0,32,64,96,128,160,192,224,256,288},{321,353,3..., dimensions={0} | all-to-all | bytes 2097152 | tf_op jit(solution)/shard_map/all_to_all | solution.py:257
  84.6 0.2 sum_aux.1
  84.9 16.9 %all_to_all.28 = bf16[32,8,128]{2,1,0:T(8,128)(2,1)S(1)} all-to-all(bf16[32,8,128]{2,1,0:T(8,128)(2,1)S(1)} %bitcast.3), channel_id=1, replica_groups={{16,17,18,19,20,21,22,23,24,25,26,27,28,29,30,31,0,1,2,3,4,5,6,7,8,9,10..., dimensions={0} | all-to-all | bytes 131072 | tf_op jit(solution)/shard_map/all_to_all | solution.py:268
  101.7 0.8 sum_planes.1
Async XLA Ops:
  2.0 22.2 %all-to-all-start = ((bf16[16,16,128]{2,1,0:T(8,128)(2,1)}), bf16[16,16,128]{2,1,0:T(8,128)(2,1)S(1)}, u32[]{:S(2)}, u32[]{:S(2)}) async-start(bf16[16,16,128]{2,1,0:T(8,128)(2,1)} %get-tuple-element.12), calls=%async_computation | async-start | bytes 131072 | tf_op jit(solution)/shard_map/all_to_all | solution.py:215
  56.1 7.1 %collective-permute-start = (bf16[16,128,512]{2,1,0:T(8,128)(2,1)S(1)}, bf16[16,128,512]{2,1,0:T(8,128)(2,1)S(1)}, u32[]{:S(2)}, u32[]{:S(2)}) collective-permute-start(bf16[16,128,512]{2,1,0:T(8,128)(2,1)S(1)} %all_to_all.26.own_ref), channel_id=1, source_target_pairs={{0,1},{1,0},{2,3},{3,2},{4,5},{5,4},{6,7},{7,6},{8,9},{9,8},{10,11... | collective-permute-start | bytes 6291464 | tf_op jit(solution)/shard_map/ppermute | solution.py:236

commit v9 on v8

--- a/solution.py
+++ b/solution.py
@@ -17,7 +17,7 @@
 PACK = 16
 PLANES = 16
 FIRST = 11
-TURN = PLANES // 2
+TURN = 9
 ROWS = 16
 SHIFT = 10
 
@@ -70,7 +70,7 @@
         scale = jnp.where(block == 0, s[0], jnp.where(block == 1, s[1], jnp.where(block == 2, s[2], s[3])))
         picks.append(jnp.where(hit, scale, 0.0).astype(jnp.bfloat16))
     most = send_ref.shape[0]
-    step = 2
+    step = 4
     for k in range(0, aux, step):
         for copy in copies[3 + k : 3 + k + step]:
             copy.wait()
@@ -173,7 +173,7 @@
     for tile in range(half):
         cores = [total(tile), total(tile + half)]
         for q in range(4):
-            slot = (tile * 4 + q + TURN) % PLANES
+            slot = (tile * 4 + q - TURN) % PLANES
             both = jnp.concatenate([gather_groups(groups, q * HALF) for groups in cores])
             out_ref[slot * PACK : (slot + 1) * PACK, :] = both.astype(out_ref.dtype)
 

time: 103 us -> 102 us (level)
  no operation moved by 1% of the time
where the time goes in v9:
time: 102 us
  blocking collectives  73 us (72%)
  starting transfers between devices  19.8 us (19%)
  Pallas kernels  5.9 us (6%)
  waiting for transfers between devices  3.39 us (3%)
    all_to_all x1, blocking collectives, body(): lax.all_to_all(slabs, ROW, 0, 0, axis_index_groups=from_corner, tiled=True)  31.6 us
    all_to_all x1, blocking collectives, body(): lax.all_to_all(partial, ROW, 0, 0, axis_index_groups=from_corner, tiled=T...  19.5 us
    all_to_all x1, blocking collectives, body(): lax.all_to_all(packed, COL, 0, 0, axis_index_groups=pairs, tiled=True)  16.7 us
    all_to_all x1, starting transfers between devices, body(): lax.all_to_all(piece, 'z', 0, 0, axis_index_groups=[late_first], tiled=True)  16.4 us
    ppermute x1, starting transfers between devices, body(): other = lax.ppermute(own, 'core', swap)  3.33 us
    ppermute x1, waiting for transfers between devices, body(): other = lax.ppermute(own, 'core', swap)  2.94 us
    all_gather x1, blocking collectives, body(): got_last = lax.all_gather(send_last, 'core', axis=0, tiled=True)  2.77 us
    all_gather x1, blocking collectives, body(): got = lax.all_gather(send, 'core', axis=0, tiled=True)  2.45 us
  transfers between devices with their start and end apart: 2, of which 2 were waited for; matrix products, arithmetic and copies ran while one was open for 0% of the time, Pallas kernels for 1%

profile of v9, /device:TPU:1, one launch (start us, length us, event | category | flops | bytes accessed | tf_op | source)
XLA Modules:
  0.0 102.1 jit_solution(6155814849518119987)
XLA Ops:
  0.0 1.8 %prepare.1 = (bf16[16,16,128]{2,1,0:T(8,128)(2,1)}, bf16[8,64,512]{2,1,0:T(8,128)(2,1)S(1)}, bf16[7,64,512]{2,1,0:T(8,128)(2,1)S(1)}, bf16[1,64,512]{2,1,0:T(8,128)(2,1)S(1)}) custom-call(bf16[8,64,1024]{2,1,0:T(8,128)(2,1)} %tc_hbm.1, bf16[32,1024]{1,0:T(8,128)(2,1)} %den_hbm.1, s32[16,16]{1,0:T(8,128)} %pair_hbm.1, s32[16,16]{1,0:T(8,128)} %dmask_hbm.1), custom_call_target="tpu_custom_call" | custom-call | tf_op jit(solution)/shard_map/prepare/pallas_call | solution.py:198
  1.8 16.4 %all-to-all-start = ((bf16[16,16,128]{2,1,0:T(8,128)(2,1)}), bf16[16,16,128]{2,1,0:T(8,128)(2,1)S(1)}, u32[]{:S(2)}, u32[]{:S(2)}) async-start(bf16[16,16,128]{2,1,0:T(8,128)(2,1)} %get-tuple-element.12), calls=%async_computation | async-start | bytes 131072 | tf_op jit(solution)/shard_map/all_to_all | solution.py:215
  18.3 2.8 %all_gather.7.last_ref = bf16[2,64,512]{2,1,0:T(8,128)(2,1)S(1)} all-gather(bf16[1,64,512]{2,1,0:T(8,128)(2,1)S(1)} %get-tuple-element.11), channel_id=1, replica_groups=mesh['y'=4,'x'=4,'z'=16,'core'=2] {'core'}, dimensions={0}, use_global_device_ids=true | all-gather | bytes 196608 | tf_op jit(solution)/shard_map/all_gather | solution.py:217
  21.0 2.4 %all_gather.6.got_ref = bf16[14,64,512]{2,1,0:T(8,128)(2,1)S(1)} all-gather(bf16[7,64,512]{2,1,0:T(8,128)(2,1)S(1)} %get-tuple-element.10), channel_id=1, replica_groups=mesh['y'=4,'x'=4,'z'=16,'core'=2] {'core'}, dimensions={0}, use_global_device_ids=true | all-gather | bytes 1376256 | tf_op jit(solution)/shard_map/all_gather | solution.py:216
  23.5 0.1 join.1.slab_ref
  23.6 0.4 all-to-all-done.den_ref
  24.0 0.3 pack.1
  24.3 31.6 %all_to_all.26.own_ref = bf16[16,128,512]{2,1,0:T(8,128)(2,1)S(1)} all-to-all(bf16[16,128,512]{2,1,0:T(8,128)(2,1)S(1)} %pack.1), channel_id=1, replica_groups={{320,352,384,416,448,480,0,32,64,96,128,160,192,224,256,288},{321,353,3..., dimensions={0} | all-to-all | bytes 4194304 | tf_op jit(solution)/shard_map/all_to_all | solution.py:235
  55.9 3.3 %collective-permute-start = (bf16[16,128,512]{2,1,0:T(8,128)(2,1)S(1)}, bf16[16,128,512]{2,1,0:T(8,128)(2,1)S(1)}, u32[]{:S(2)}, u32[]{:S(2)}) collective-permute-start(bf16[16,128,512]{2,1,0:T(8,128)(2,1)S(1)} %all_to_all.26.own_ref), channel_id=1, source_target_pairs={{0,1},{1,0},{2,3},{3,2},{4,5},{5,4},{6,7},{7,6},{8,9},{9,8},{10,11... | collective-permute-start | bytes 6291464 | tf_op jit(solution)/shard_map/ppermute | solution.py:236
  59.3 0.8 begin.1.sum_ref
  60.1 2.9 %collective-permute-done.other_ref = bf16[16,128,512]{2,1,0:T(8,128)(2,1)S(1)} collective-permute-done((bf16[16,128,512]{2,1,0:T(8,128)(2,1)S(1)}, bf16[16,128,512]{2,1,0:T(8,128)(2,1)S(1)}, u32[]{:S(2)}, u32[]{:S(2)}) %collective-permute-start) | collective-permute-done | bytes 2097184 | tf_op jit(solution)/shard_map/ppermute | solution.py:236
  63.0 1.9 %contract.1 = bf16[16,32,1024]{2,1,0:T(8,128)(2,1)S(1)} custom-call(bf16[16,128,512]{2,1,0:T(8,128)(2,1)S(1)} %all_to_all.26.own_ref, bf16[16,128,512]{2,1,0:T(8,128)(2,1)S(1)} %collective-permute-done.other_ref, f32[512,1024]{1,0:T(8,128)S(1)} %begin.1.sum_ref), custom_call_target="tpu_custom_call" | custom-call | tf_op jit(solution)/shard_map/contract/pallas_call | solution.py:248
  65.0 19.5 %all_to_all.27.in_ref = bf16[16,32,1024]{2,1,0:T(8,128)(2,1)S(1)} all-to-all(bf16[16,32,1024]{2,1,0:T(8,128)(2,1)S(1)} %contract.1), channel_id=1, replica_groups={{320,352,384,416,448,480,0,32,64,96,128,160,192,224,256,288},{321,353,3..., dimensions={0} | all-to-all | bytes 2097152 | tf_op jit(solution)/shard_map/all_to_all | solution.py:257
  84.4 0.2 sum_aux.1
  84.7 16.7 %all_to_all.28 = bf16[32,8,128]{2,1,0:T(8,128)(2,1)S(1)} all-to-all(bf16[32,8,128]{2,1,0:T(8,128)(2,1)S(1)} %bitcast.3), channel_id=1, replica_groups={{18,19,20,21,22,23,24,25,26,27,28,29,30,31,0,1,2,3,4,5,6,7,8,9,10,11,12..., dimensions={0} | all-to-all | bytes 131072 | tf_op jit(solution)/shard_map/all_to_all | solution.py:268
  101.3 0.8 sum_planes.1
Async XLA Ops:
  1.8 22.2 %all-to-all-start = ((bf16[16,16,128]{2,1,0:T(8,128)(2,1)}), bf16[16,16,128]{2,1,0:T(8,128)(2,1)S(1)}, u32[]{:S(2)}, u32[]{:S(2)}) async-start(bf16[16,16,128]{2,1,0:T(8,128)(2,1)} %get-tuple-element.12), calls=%async_computation | async-start | bytes 131072 | tf_op jit(solution)/shard_map/all_to_all | solution.py:215
  55.9 7.1 %collective-permute-start = (bf16[16,128,512]{2,1,0:T(8,128)(2,1)S(1)}, bf16[16,128,512]{2,1,0:T(8,128)(2,1)S(1)}, u32[]{:S(2)}, u32[]{:S(2)}) collective-permute-start(bf16[16,128,512]{2,1,0:T(8,128)(2,1)S(1)} %all_to_all.26.own_ref), channel_id=1, source_target_pairs={{0,1},{1,0},{2,3},{3,2},{4,5},{5,4},{6,7},{7,6},{8,9},{9,8},{10,11... | collective-permute-start | bytes 6291464 | tf_op jit(solution)/shard_map/ppermute | solution.py:236

commit v10 on v9

--- a/solution.py
+++ b/solution.py
@@ -16,7 +16,7 @@
 LANES = 128
 PACK = 16
 PLANES = 16
-FIRST = 11
+FIRST = 10
 TURN = 9
 ROWS = 16
 SHIFT = 10

time: 102 us -> 103 us (level)
  transfers between devices with their start and end apart: 2 -> 2, of which waited for: 2 -> 1; matrix products, arithmetic and copies ran while one was open for 0% -> 0% of each run, Pallas kernels for 1% -> 1%
where the time goes in v10:
time: 103 us
  blocking collectives  73.5 us (71%)
  starting transfers between devices  20.5 us (20%)
  Pallas kernels  5.9 us (6%)
  waiting for transfers between devices  2.94 us (3%)
    all_to_all x1, blocking collectives, body(): lax.all_to_all(slabs, ROW, 0, 0, axis_index_groups=from_corner, tiled=True)  31.6 us
    all_to_all x1, blocking collectives, body(): lax.all_to_all(partial, ROW, 0, 0, axis_index_groups=from_corner, tiled=T...  19.3 us
    all_to_all x1, blocking collectives, body(): lax.all_to_all(packed, COL, 0, 0, axis_index_groups=pairs, tiled=True)  17.4 us
    all_to_all x1, starting transfers between devices, body(): lax.all_to_all(piece, 'z', 0, 0, axis_index_groups=[late_first], tiled=True)  17.3 us
    ppermute x1, starting transfers between devices, body(): other = lax.ppermute(own, 'core', swap)  3.13 us
    ppermute x1, waiting for transfers between devices, body(): other = lax.ppermute(own, 'core', swap)  2.94 us
    all_gather x1, blocking collectives, body(): got_last = lax.all_gather(send_last, 'core', axis=0, tiled=True)  2.77 us
    all_gather x1, blocking collectives, body(): got = lax.all_gather(send, 'core', axis=0, tiled=True)  2.45 us
  transfers between devices with their start and end apart: 2, of which 1 were waited for; matrix products, arithmetic and copies ran while one was open for 0% of the time, Pallas kernels for 1%

profile of v10, /device:TPU:1, one launch (start us, length us, event | category | flops | bytes accessed | tf_op | source)
XLA Modules:
  0.0 102.8 jit_solution(11950145077086878234)
XLA Ops:
  0.0 1.8 %prepare.1 = (bf16[16,16,128]{2,1,0:T(8,128)(2,1)}, bf16[8,64,512]{2,1,0:T(8,128)(2,1)S(1)}, bf16[7,64,512]{2,1,0:T(8,128)(2,1)S(1)}, bf16[1,64,512]{2,1,0:T(8,128)(2,1)S(1)}) custom-call(bf16[8,64,1024]{2,1,0:T(8,128)(2,1)} %tc_hbm.1, bf16[32,1024]{1,0:T(8,128)(2,1)} %den_hbm.1, s32[16,16]{1,0:T(8,128)} %pair_hbm.1, s32[16,16]{1,0:T(8,128)} %dmask_hbm.1), custom_call_target="tpu_custom_call" | custom-call | tf_op jit(solution)/shard_map/prepare/pallas_call | solution.py:198
  1.8 17.3 %all-to-all-start = ((bf16[16,16,128]{2,1,0:T(8,128)(2,1)}), bf16[16,16,128]{2,1,0:T(8,128)(2,1)S(1)}, u32[]{:S(2)}, u32[]{:S(2)}) async-start(bf16[16,16,128]{2,1,0:T(8,128)(2,1)} %get-tuple-element.12), calls=%async_computation | async-start | bytes 131072 | tf_op jit(solution)/shard_map/all_to_all | solution.py:215
  19.2 2.8 %all_gather.7.last_ref = bf16[2,64,512]{2,1,0:T(8,128)(2,1)S(1)} all-gather(bf16[1,64,512]{2,1,0:T(8,128)(2,1)S(1)} %get-tuple-element.11), channel_id=1, replica_groups=mesh['y'=4,'x'=4,'z'=16,'core'=2] {'core'}, dimensions={0}, use_global_device_ids=true | all-gather | bytes 196608 | tf_op jit(solution)/shard_map/all_gather | solution.py:217
  21.9 2.4 %all_gather.6.got_ref = bf16[14,64,512]{2,1,0:T(8,128)(2,1)S(1)} all-gather(bf16[7,64,512]{2,1,0:T(8,128)(2,1)S(1)} %get-tuple-element.10), channel_id=1, replica_groups=mesh['y'=4,'x'=4,'z'=16,'core'=2] {'core'}, dimensions={0}, use_global_device_ids=true | all-gather | bytes 1376256 | tf_op jit(solution)/shard_map/all_gather | solution.py:216
  24.4 0.1 join.1.slab_ref
  24.5 0.0 all-to-all-done.den_ref
  24.5 0.3 pack.1
  24.8 31.6 %all_to_all.26.own_ref = bf16[16,128,512]{2,1,0:T(8,128)(2,1)S(1)} all-to-all(bf16[16,128,512]{2,1,0:T(8,128)(2,1)S(1)} %pack.1), channel_id=1, replica_groups={{320,352,384,416,448,480,0,32,64,96,128,160,192,224,256,288},{321,353,3..., dimensions={0} | all-to-all | bytes 4194304 | tf_op jit(solution)/shard_map/all_to_all | solution.py:235
  56.3 3.1 %collective-permute-start = (bf16[16,128,512]{2,1,0:T(8,128)(2,1)S(1)}, bf16[16,128,512]{2,1,0:T(8,128)(2,1)S(1)}, u32[]{:S(2)}, u32[]{:S(2)}) collective-permute-start(bf16[16,128,512]{2,1,0:T(8,128)(2,1)S(1)} %all_to_all.26.own_ref), channel_id=1, source_target_pairs={{0,1},{1,0},{2,3},{3,2},{4,5},{5,4},{6,7},{7,6},{8,9},{9,8},{10,11... | collective-permute-start | bytes 6291464 | tf_op jit(solution)/shard_map/ppermute | solution.py:236
  59.5 0.8 begin.1.sum_ref
  60.3 2.9 %collective-permute-done.other_ref = bf16[16,128,512]{2,1,0:T(8,128)(2,1)S(1)} collective-permute-done((bf16[16,128,512]{2,1,0:T(8,128)(2,1)S(1)}, bf16[16,128,512]{2,1,0:T(8,128)(2,1)S(1)}, u32[]{:S(2)}, u32[]{:S(2)}) %collective-permute-start) | collective-permute-done | bytes 2097184 | tf_op jit(solution)/shard_map/ppermute | solution.py:236
  63.2 1.9 %contract.1 = bf16[16,32,1024]{2,1,0:T(8,128)(2,1)S(1)} custom-call(bf16[16,128,512]{2,1,0:T(8,128)(2,1)S(1)} %all_to_all.26.own_ref, bf16[16,128,512]{2,1,0:T(8,128)(2,1)S(1)} %collective-permute-done.other_ref, f32[512,1024]{1,0:T(8,128)S(1)} %begin.1.sum_ref), custom_call_target="tpu_custom_call" | custom-call | tf_op jit(solution)/shard_map/contract/pallas_call | solution.py:248
  65.2 19.3 %all_to_all.27.in_ref = bf16[16,32,1024]{2,1,0:T(8,128)(2,1)S(1)} all-to-all(bf16[16,32,1024]{2,1,0:T(8,128)(2,1)S(1)} %contract.1), channel_id=1, replica_groups={{320,352,384,416,448,480,0,32,64,96,128,160,192,224,256,288},{321,353,3..., dimensions={0} | all-to-all | bytes 2097152 | tf_op jit(solution)/shard_map/all_to_all | solution.py:257
  84.5 0.2 sum_aux.1
  84.7 17.4 %all_to_all.28 = bf16[32,8,128]{2,1,0:T(8,128)(2,1)S(1)} all-to-all(bf16[32,8,128]{2,1,0:T(8,128)(2,1)S(1)} %bitcast.3), channel_id=1, replica_groups={{18,19,20,21,22,23,24,25,26,27,28,29,30,31,0,1,2,3,4,5,6,7,8,9,10,11,12..., dimensions={0} | all-to-all | bytes 131072 | tf_op jit(solution)/shard_map/all_to_all | solution.py:268
  102.1 0.8 sum_planes.1
Async XLA Ops:
  1.8 22.6 %all-to-all-start = ((bf16[16,16,128]{2,1,0:T(8,128)(2,1)}), bf16[16,16,128]{2,1,0:T(8,128)(2,1)S(1)}, u32[]{:S(2)}, u32[]{:S(2)}) async-start(bf16[16,16,128]{2,1,0:T(8,128)(2,1)} %get-tuple-element.12), calls=%async_computation | async-start | bytes 131072 | tf_op jit(solution)/shard_map/all_to_all | solution.py:215
  56.3 6.9 %collective-permute-start = (bf16[16,128,512]{2,1,0:T(8,128)(2,1)S(1)}, bf16[16,128,512]{2,1,0:T(8,128)(2,1)S(1)}, u32[]{:S(2)}, u32[]{:S(2)}) collective-permute-start(bf16[16,128,512]{2,1,0:T(8,128)(2,1)S(1)} %all_to_all.26.own_ref), channel_id=1, source_target_pairs={{0,1},{1,0},{2,3},{3,2},{4,5},{5,4},{6,7},{7,6},{8,9},{9,8},{10,11... | collective-permute-start | bytes 6291464 | tf_op jit(solution)/shard_map/ppermute | solution.py:236
